TPU v7x, 32 devices: a whole 2x2x4 slice. The times are simulated.
32 devices in a mesh: prow: 4 (over x, core), pcol: 8 (over z, y).
Axes of the slice: x: 2, y: 2, z: 4, core: 2. Of those that a mesh axis runs over, the one named last changes fastest.
Arguments:
- diag_block: float32 [512, 512], P('prow'), as said below
- panel_cols: float32 [8192, 512], P(('prow', 'pcol')), may hold values from -3 to 3
- trailing: float32 [8192, 8192], P('prow', 'pcol'), may hold values from -6 to 6
- geno_top: float32 [512, 2048], P('prow', 'pcol'), may hold values from -6 to 6
- geno_rest: float32 [8192, 2048], P('prow', 'pcol'), may hold values from -6 to 6
- pheno_top: float32 [512], P('prow'), may hold values from -6 to 6
- pheno_rest: float32 [8192], P('prow'), may hold values from -6 to 6
Outputs:
- updated_block: float32 [8192, 8192], P('prow', 'pcol')
- panel_factor: float32 [8192, 512], P(('prow', 'pcol'))
- white_geno: float32 [8192, 2048], P('prow', 'pcol')
- score_stat: float32 [2048], P('pcol')
- info_stat: float32 [2048], P('pcol')
Inputs may be any that keep to these rules, and one draw needn't show every extreme that they name: diag_block is symmetric and positive definite; its diagonal entries lie between 3 and 4.5 and its off-diagonal entries have magnitude at most 0.8.
All inputs are finite; a program needn't handle non-finite values.
Results may differ from a plain program's by a relative error of at most 0.000096.
Values sent between devices are 32-bit elements; how exact they have to be, the bound alone decides.
A program may use at most 64 MiB of HBM per device.

v0:
```python
import functools

import jax
import jax.numpy as jnp
from jax import lax
from jax.experimental import pallas as pl
from jax.experimental.pallas import tpu as pltpu
from jax.sharding import PartitionSpec as P

MESH = pl.DeviceIdType.MESH
HIGHEST = lax.Precision.HIGHEST
TILE = 16
PARTS = 4
BLOCK = 128


def split3(value):
    hi = value.astype(jnp.bfloat16).astype(jnp.float32)
    rest = value - hi
    mid = rest.astype(jnp.bfloat16).astype(jnp.float32)
    return hi, mid, rest - mid


def tile_step(m_ref, step):
    start = pl.multiple_of(step * TILE, TILE)
    left = m_ref[pl.ds(start, TILE), :BLOCK]
    right = m_ref[pl.ds(start, TILE), BLOCK:]
    rolled = pltpu.roll(left, lax.rem(BLOCK - start, BLOCK), 1)
    cols = [jnp.broadcast_to(rolled[:, k : k + 1], (TILE, BLOCK)) for k in range(TILE)]
    rows = lax.broadcasted_iota(jnp.int32, (TILE, BLOCK), 0)
    lanes = lax.broadcasted_iota(jnp.int32, (TILE, BLOCK), 1)
    pivots = jnp.zeros_like(left)
    for j in range(TILE):
        pivot = jnp.broadcast_to(cols[j][j : j + 1, :], (TILE, BLOCK))
        inv = pl.reciprocal(pivot, approx=True)
        inv = inv * (2.0 - pivot * inv)
        below = jnp.where(rows > j, cols[j], 0.0)
        pivots = jnp.where(rows == j, pivot, pivots)

        def work(value):
            return value - below * (jnp.broadcast_to(value[j : j + 1, :], (TILE, BLOCK)) * inv)

        for k in range(j + 1, TILE):
            cols[k] = work(cols[k])
        left, right = work(left), work(right)
    scale = lax.rsqrt(pivots)
    scale = scale * (1.5 - (0.5 * pivots) * scale * scale)
    left, right = left * scale, right * scale
    m_ref[pl.ds(start, TILE), :BLOCK] = left
    m_ref[pl.ds(start, TILE), BLOCK:] = right
    both = jnp.concatenate([left, right], axis=1)
    mult = jnp.where(lanes >= start + TILE, left, 0.0)
    a0, a1, a2 = split3(mult)
    b0, b1, b2 = split3(both)
    lhs = jnp.concatenate([a0, a0, a1, a0, a1, a2], axis=0).astype(jnp.bfloat16)
    rhs = jnp.concatenate([b0, b1, b0, b2, b1, b0], axis=0).astype(jnp.bfloat16)
    m_ref[...] -= lax.dot_general(
        lhs, rhs, (((0,), (0,)), ((), ())), preferred_element_type=jnp.float32
    )


def dot_t(a, b):
    return lax.dot_general(
        a, b, (((0,), (0,)), ((), ())), precision=HIGHEST, preferred_element_type=jnp.float32
    )


def dot_n(a, b):
    return jnp.dot(a, b, precision=HIGHEST, preferred_element_type=jnp.float32)


def invert(a_ref, w_ref, m_ref, events):
    width = a_ref.shape[0]
    blocks = width // BLOCK
    tiles = BLOCK // TILE
    w_ref[...] = jnp.zeros_like(w_ref)
    eye = (
        lax.broadcasted_iota(jnp.int32, (BLOCK, BLOCK), 0)
        == lax.broadcasted_iota(jnp.int32, (BLOCK, BLOCK), 1)
    ).astype(jnp.float32)
    slot = 0
    for k in range(blocks):
        lo, hi = k * BLOCK, (k + 1) * BLOCK
        m_ref[:, :BLOCK] = a_ref[lo:hi, lo:hi]
        m_ref[:, BLOCK:] = eye
        for part in range(PARTS):

            def body(step, carry):
                tile_step(m_ref, step)
                return carry

            lax.fori_loop(part * tiles // PARTS, (part + 1) * tiles // PARTS, body, 0)
            if part < PARTS - 1:
                if slot < len(events):
                    events[slot]()
                slot += 1
        own = m_ref[:, BLOCK:]
        if k > 0:
            w_ref[lo:hi, :lo] = dot_n(own, w_ref[lo:hi, :lo])
        w_ref[lo:hi, lo:hi] = own
        if k < blocks - 1:
            upper = dot_n(own, a_ref[lo:hi, hi:])
            a_ref[hi:, hi:] -= dot_t(upper, upper)
            w_ref[hi:, :hi] -= dot_t(upper, w_ref[lo:hi, :hi])
        if slot < len(events):
            events[slot]()
        slot += 1
    while slot < len(events):
        events[slot]()
        slot += 1


def gather_kernel(
    ly, lz, group,
    diag_in, top_in, pheno_in, panel_in,
    w_out, row_out, col_out, top_out, pheno_out,
    a_ref, m_ref,
    small_send, small_recv, row_send, row_recv, col_send, col_recv, local_sem,
):
    r, c = lax.axis_index("prow"), lax.axis_index("pcol")
    z, y = c // ly, lax.rem(c, ly)
    sib = r + 1 - 2 * lax.rem(r, 2)
    cross = r + 2 - 4 * (r // 2)
    diag_x = sib + 2 - 4 * (sib // 2)
    other = z * ly + (1 - y)
    col_parts = col_out.shape[0]
    root = c // group
    first = lax.rem(c, group) * col_parts
    is_root = root == r
    root_cross = root + 2 - 4 * (root // 2)

    barrier = pltpu.get_barrier_semaphore()

    def greet(row, col):
        pl.semaphore_signal(barrier, inc=1, device_id={"prow": row, "pcol": col}, device_id_type=MESH)

    greet(sib, c)
    greet(cross, c)
    greet(r, other)

    @pl.when(z > 0)
    def _():
        greet(r, c - ly)

    @pl.when(z < lz - 1)
    def _():
        greet(r, c + ly)

    pl.semaphore_wait(barrier, 3 + jnp.minimum(z, 1) + jnp.minimum(lz - 1 - z, 1))

    def remote(src, dst, send, recv, row, col):
        return pltpu.make_async_remote_copy(
            src_ref=src, dst_ref=dst, send_sem=send, recv_sem=recv,
            device_id={"prow": row, "pcol": col}, device_id_type=MESH,
        )

    height = diag_in.shape[0]

    def diag_at(q):
        return a_ref.at[pl.ds(pl.multiple_of(q * height, height), height), :]

    places = (diag_at, lambda q: top_out.at[q], lambda q: pheno_out.at[q])

    def small(kind, lane):
        source = (diag_in, top_in, pheno_in)[kind]
        place = places[kind]
        part = cross if lane == 2 else r
        src = place(part) if lane == 2 else source
        return remote(
            src, place(part), small_send.at[kind, lane], small_recv.at[kind, part],
            cross if lane == 1 else sib, c,
        )

    def small_wait(kind, part):
        place = places[kind]
        remote(place(part), place(part), small_send.at[kind, 0], small_recv.at[kind, part], sib, c).wait_recv()

    def row_copy(way, b, own):
        target = (c + ly, c - ly, other)[way]
        return remote(
            panel_in if own else row_out.at[b], row_out.at[b],
            row_send.at[way, b], row_recv.at[b], r, target,
        )

    def row_wait(b):
        remote(row_out.at[b], row_out.at[b], row_send.at[0, b], row_recv.at[b], r, other).wait_recv()

    def col_copies(b, own):
        i = b - first
        src = panel_in if own else row_out.at[b]
        return (
            remote(src, col_out.at[i], col_send.at[0, i], col_recv.at[i], cross, c),
            remote(src, col_out.at[i], col_send.at[1, i], col_recv.at[i], sib, c),
            pltpu.make_async_copy(src, col_out.at[i], local_sem.at[1 + i]),
        )

    def in_col(b):
        return is_root & (b >= first) & (b < first + col_parts)

    def col_start(b, own):
        @pl.when(in_col(b))
        def _():
            for copy in col_copies(b, own):
                copy.start()

    def col_finish(b, own):
        @pl.when(in_col(b))
        def _():
            one, two, three = col_copies(b, own)
            one.wait_send()
            two.wait_send()
            three.wait()

    def up(fn):
        pl.when(z < lz - 1)(fn)

    def down(fn):
        pl.when(z > 0)(fn)

    small(0, 1).start()
    small(0, 0).start()
    row_copy(2, c, True).start()
    up(lambda: row_copy(0, c, True).start())
    down(lambda: row_copy(1, c, True).start())
    for kind in (1, 2):
        small(kind, 1).start()
        small(kind, 0).start()
    own_copy = pltpu.make_async_copy(panel_in, row_out.at[c], local_sem.at[0])
    own_copy.start()
    top_copy = pltpu.make_async_copy(top_in, top_out.at[r], local_sem.at[1 + col_parts])
    top_copy.start()
    pheno_copy = pltpu.make_async_copy(pheno_in, pheno_out.at[r], local_sem.at[2 + col_parts])
    pheno_copy.start()
    diag_copy = pltpu.make_async_copy(diag_in, diag_at(r), local_sem.at[3 + col_parts])
    diag_copy.start()
    col_start(c, True)
    small_wait(0, cross)
    small(0, 2).start()
    small_wait(0, sib)
    small_wait(0, diag_x)
    diag_copy.wait()
    small(0, 2).wait_send()

    def hop(d):
        low, high = c - d * ly, c + d * ly

        @pl.when(z >= d)
        def _():
            row_wait(low)
            up(lambda: row_copy(0, low, False).start())
            row_copy(2, low, False).start()
            col_start(low, False)

        @pl.when(z + d < lz)
        def _():
            row_wait(high)
            down(lambda: row_copy(1, high, False).start())
            row_copy(2, high, False).start()
            col_start(high, False)

    def across(d):
        def one(b):
            row_wait(b)
            col_start(b, False)

        if d == 0:
            one(other)
        else:
            pl.when(z >= d)(lambda: one(other - d * ly))
            pl.when(z + d < lz)(lambda: one(other + d * ly))

    def top_event():
        for kind in (1, 2):
            small_wait(kind, cross)
            small(kind, 2).start()

    def nothing():
        pass

    def hop_at(d):
        return functools.partial(hop, d) if d < lz else nothing

    def across_at(d):
        return functools.partial(across, d) if d < lz else nothing

    events = [hop_at(1), across_at(0), top_event, nothing, hop_at(2), nothing, nothing, nothing]
    events += [nothing, across_at(1), hop_at(3), nothing, nothing, across_at(2), nothing, nothing]
    for d in range(4, lz):
        events += [hop_at(d), across_at(d - 1)]
    events.append(across_at(lz - 1))
    invert(a_ref, w_out, m_ref, events)

    def handed(i):
        return remote(col_out.at[i], col_out.at[i], col_send.at[1, i], col_recv.at[i], sib, c)

    @pl.when(r == root_cross)
    def _():
        for i in range(col_parts):
            handed(i).wait_recv()
            handed(i).start()
        for i in range(col_parts):
            handed(i).wait_send()

    @pl.when(jnp.logical_not(is_root) & (r != root_cross))
    def _():
        for i in range(col_parts):
            handed(i).wait_recv()

    small(0, 1).wait_send()
    small(0, 0).wait_send()
    for kind in (1, 2):
        for lane in range(3):
            small(kind, lane).wait_send()
        small_wait(kind, sib)
        small_wait(kind, diag_x)
    own_copy.wait()
    top_copy.wait()
    pheno_copy.wait()
    row_copy(2, c, True).wait_send()
    up(lambda: row_copy(0, c, True).wait_send())
    down(lambda: row_copy(1, c, True).wait_send())
    col_finish(c, True)
    col_finish(other, False)
    for d in range(1, lz):

        @pl.when(z >= d)
        def _():
            low = c - d * ly
            up(lambda: row_copy(0, low, False).wait_send())
            row_copy(2, low, False).wait_send()
            col_finish(low, False)
            col_finish(other - d * ly, False)

        @pl.when(z + d < lz)
        def _():
            high = c + d * ly
            down(lambda: row_copy(1, high, False).wait_send())
            row_copy(2, high, False).wait_send()
            col_finish(high, False)
            col_finish(other + d * ly, False)


def gather_and_invert(diag_block, geno_top, pheno_row, panel_cols, prow_size, pcol_size):
    ly = 2
    lz = pcol_size // ly
    height, width = diag_block.shape
    rows_piece = panel_cols.shape[0]
    col_parts = prow_size
    any_spec = pl.BlockSpec(memory_space=pl.ANY)
    vmem = pl.BlockSpec(memory_space=pltpu.VMEM)
    dma = pltpu.SemaphoreType.DMA
    f32 = jnp.float32
    return pl.pallas_call(
        functools.partial(gather_kernel, ly, lz, pcol_size // prow_size),
        out_shape=(
            jax.ShapeDtypeStruct((width, width), f32),
            jax.ShapeDtypeStruct((pcol_size, rows_piece, width), f32),
            jax.ShapeDtypeStruct((col_parts, rows_piece, width), f32),
            jax.ShapeDtypeStruct((prow_size,) + geno_top.shape, f32),
            jax.ShapeDtypeStruct((prow_size,) + pheno_row.shape, f32),
        ),
        in_specs=[pl.BlockSpec(memory_space=pltpu.HBM)] * 4,
        out_specs=(vmem, any_spec, any_spec, any_spec, any_spec),
        scratch_shapes=[
            pltpu.VMEM((width, width), f32),
            pltpu.VMEM((BLOCK, 2 * BLOCK), f32),
            dma((3, 3)),
            dma((3, prow_size)),
            dma((3, pcol_size)),
            dma((pcol_size,)),
            dma((2, col_parts)),
            dma((col_parts,)),
            dma((4 + col_parts,)),
        ],
        compiler_params=pltpu.CompilerParams(
            collective_id=0, has_side_effects=True, vmem_limit_bytes=24 * 1024 * 1024
        ),
    )(diag_block, geno_top, pheno_row, panel_cols)


LAST = ((1,), (1,))
INNER = ((1,), (0,))


def split2(value):
    hi = value.astype(jnp.bfloat16)
    return hi, (value - hi.astype(jnp.float32)).astype(jnp.bfloat16)


def dot3(a, b, dims):
    left = jnp.concatenate([a[0], a[0], a[1]], axis=dims[0][0])
    right = jnp.concatenate([b[0], b[1], b[0]], axis=dims[1][0])
    return lax.dot_general(left, right, (dims, ((), ())), preferred_element_type=jnp.float32)


def column(row):
    return jnp.transpose(jnp.broadcast_to(row, (BLOCK, row.shape[1])))


def weighted(weights, values):
    wide = jnp.concatenate([weights] * (values.shape[1] // BLOCK), axis=1)
    return jnp.sum(wide * values, axis=0, keepdims=True)


def whiten_kernel(
    tile, pieces, col_tiles,
    w_in, top_in, pheno_in, rows_in, cols_in, geno_in, rest_in,
    hi_out, lo_out, col_hi_out, col_lo_out, own_out, geno_out, stat_out,
    w_hi, w_lo, turned_hi, turned_lo, top_hi, top_lo, kept,
):
    step = pl.program_id(0)
    place = lax.axis_index("pcol") * own_out.shape[0]
    variants = geno_in.shape[1]

    @pl.when(step == 0)
    def _():
        w_hi[...], w_lo[...] = split2(w_in[...])
        w = (w_hi[...], w_lo[...])
        turned_hi[...], turned_lo[...] = split2(jnp.transpose(w_in[...]))
        joined = jnp.concatenate([top_in[...], column(pheno_in[...])], axis=1)
        both = dot3(w, split2(joined), INNER)
        top_hi[...], top_lo[...] = split2(both)
        white = both[:, :variants]
        stat_out[...] = jnp.zeros_like(stat_out)
        stat_out[2:3, :] = weighted(both[:, variants:], white)
        stat_out[3:4, :] = jnp.sum(white * white, axis=0, keepdims=True)

    w = (w_hi[...], w_lo[...])
    panel = dot3(split2(rows_in[...]), (turned_hi[...], turned_lo[...]), INNER)
    parts = split2(panel)
    hi_out[...], lo_out[...] = parts

    @pl.when(place // tile == step)
    def _():
        kept[...] = panel
        start = pl.multiple_of(lax.rem(place, tile), TILE)
        own_out[...] = kept[pl.ds(start, own_out.shape[0]), :]

    @pl.when(step < col_tiles)
    def _():
        col_hi_out[...], col_lo_out[...] = split2(dot3(w, split2(cols_in[...]), LAST))

    shift = dot3(parts, (top_hi[...], top_lo[...]), INNER)
    white = geno_in[...] - shift[:, :variants]
    geno_out[...] = white
    stat_out[0:1, :] += weighted(column(rest_in[0]) - shift[:, variants:], white)
    stat_out[1:2, :] += jnp.sum(white * white, axis=0, keepdims=True)


def whiten(inverse, top, pheno, rows, cols, geno_rest, pheno_rest, rows_piece):
    width = inverse.shape[0]
    row_count, variants = geno_rest.shape
    col_count = cols.shape[0]
    tile = min(256, row_count)
    col_tile = min(256, col_count)
    steps, col_tiles = row_count // tile, col_count // col_tile
    f32, bf16 = jnp.float32, jnp.bfloat16
    rest = pheno_rest.reshape(steps, 1, tile)

    def fixed(shape):
        return pl.BlockSpec(shape, lambda i: (0,) * len(shape))

    def by_row(wide):
        return pl.BlockSpec((tile, wide), lambda i: (i, 0))

    last = col_tiles - 1
    col_out = pl.BlockSpec((width, col_tile), lambda i: (0, jnp.minimum(i, last)))
    return pl.pallas_call(
        functools.partial(whiten_kernel, tile, rows_piece, col_tiles),
        grid=(steps,),
        in_specs=[
            fixed((width, width)),
            fixed((width, variants)),
            fixed((1, width)),
            by_row(width),
            pl.BlockSpec((col_tile, width), lambda i: (jnp.minimum(i, last), 0)),
            by_row(variants),
            pl.BlockSpec((1, 1, tile), lambda i: (i, 0, 0)),
        ],
        out_specs=(
            by_row(width), by_row(width), col_out, col_out,
            fixed((rows_piece, width)), by_row(variants), fixed((8, variants)),
        ),
        out_shape=(
            jax.ShapeDtypeStruct((row_count, width), bf16),
            jax.ShapeDtypeStruct((row_count, width), bf16),
            jax.ShapeDtypeStruct((width, col_count), bf16),
            jax.ShapeDtypeStruct((width, col_count), bf16),
            jax.ShapeDtypeStruct((rows_piece, width), f32),
            jax.ShapeDtypeStruct((row_count, variants), f32),
            jax.ShapeDtypeStruct((8, variants), f32),
        ),
        scratch_shapes=[
            pltpu.VMEM((width, width), bf16),
            pltpu.VMEM((width, width), bf16),
            pltpu.VMEM((width, width), bf16),
            pltpu.VMEM((width, width), bf16),
            pltpu.VMEM((width, variants + BLOCK), bf16),
            pltpu.VMEM((width, variants + BLOCK), bf16),
            pltpu.VMEM((tile, width), f32),
        ],
        compiler_params=pltpu.CompilerParams(vmem_limit_bytes=20 * 1024 * 1024),
        cost_estimate=pl.CostEstimate(
            flops=6 * width * width * (row_count + col_count),
            bytes_accessed=16 * 1024 * 1024,
            transcendentals=0,
        ),
    )(inverse, top, pheno, rows, cols, geno_rest, rest)


def update_kernel(hi_in, lo_in, col_hi_in, col_lo_in, trailing_in, out):
    right = (col_hi_in[...], col_lo_in[...])
    out[...] = trailing_in[...] - dot3((hi_in[...], lo_in[...]), right, INNER)


def update(hi, lo, col_hi, col_lo, trailing):
    row_count, col_count = trailing.shape
    width = hi.shape[1]
    tile = min(256, row_count)
    left = pl.BlockSpec((tile, width), lambda i: (i, 0))
    right = pl.BlockSpec((width, col_count), lambda i: (0, 0))
    block = pl.BlockSpec((tile, col_count), lambda i: (i, 0))
    return pl.pallas_call(
        update_kernel,
        grid=(row_count // tile,),
        in_specs=[left, left, right, right, block],
        out_specs=block,
        out_shape=jax.ShapeDtypeStruct(trailing.shape, jnp.float32),
        compiler_params=pltpu.CompilerParams(vmem_limit_bytes=20 * 1024 * 1024),
        cost_estimate=pl.CostEstimate(
            flops=6 * width * row_count * col_count,
            bytes_accessed=20 * 1024 * 1024,
            transcendentals=0,
        ),
    )(hi, lo, col_hi, col_lo, trailing)


def local(diag_block, panel_cols, trailing, geno_top, geno_rest, pheno_top, pheno_rest):
    prow_size, pcol_size = lax.axis_size("prow"), lax.axis_size("pcol")
    height, width = diag_block.shape
    rows_piece = panel_cols.shape[0]
    row_count = rows_piece * pcol_size
    variants = geno_top.shape[1]
    inverse, whole, col_raw, top_all, pheno_all = gather_and_invert(
        diag_block, geno_top, pheno_top.reshape(1, height), panel_cols, prow_size, pcol_size
    )
    hi, lo, col_hi, col_lo, own_factor, white_geno, stats = whiten(
        inverse,
        top_all.reshape(width, variants),
        pheno_all.reshape(1, width),
        whole.reshape(row_count, width),
        col_raw.reshape(-1, width),
        geno_rest,
        pheno_rest,
        rows_piece,
    )

    def fetch(flip):
        return lax.ppermute(stats, "prow", [(i, i ^ flip) for i in range(prow_size)])

    sib, cross, diag = fetch(1), fetch(2), fetch(3)
    updated_block = update(hi, lo, col_hi, col_lo, trailing)
    total = (stats + sib) + (cross + diag)
    count = jnp.float32(width + row_count * prow_size)
    score_stat = (total[0] + stats[2]) / jnp.sqrt(count)
    info_stat = (total[1] + stats[3]) / count
    return (updated_block, own_factor, white_geno, score_stat, info_stat)


def solution(mesh):
    placed = (
        P("prow", None),
        P(("prow", "pcol"), None),
        P("prow", "pcol"),
        P("prow", "pcol"),
        P("prow", "pcol"),
        P("prow"),
        P("prow"),
    )
    return jax.shard_map(
        local,
        mesh=mesh,
        in_specs=placed,
        out_specs=(
            P("prow", "pcol"),
            P(("prow", "pcol"), None),
            P("prow", "pcol"),
            P("pcol"),
            P("pcol"),
        ),
        check_vma=False,
    )
```

profile of v0, /device:TPU:7, one launch (start us, length us, event | category | flops | bytes accessed | tf_op | source)
XLA Modules:
  0.0 95.5 jit_solution(5535047209147485731)
XLA Ops:
  0.6 0.0 copy-start
  0.6 1.0 %copy-done = f32[256,512]{1,0:T(8,128)S(1)} copy-done((f32[256,512]{1,0:T(8,128)S(1)}, f32[256,512]{1,0:T(8,128)}, u32[]{:S(2)}) %copy-start) | copy-done | bytes 524312
  1.7 0.0 copy-start.1
  1.7 0.9 copy-done.1
  2.6 0.0 copy-start.2
  2.6 0.9 copy-done.2
  3.5 0.0 copy-start.3
  3.5 0.7 copy-done.3
  4.2 0.0 slice-start
  4.2 61.9 %shard_map.110 = (f32[512,512]{1,0:T(8,128)S(1)}, f32[8,256,512]{2,1,0:T(8,128)S(1)}, f32[4,256,512]{2,1,0:T(8,128)S(1)}, f32[4,128,256]{2,1,0:T(8,128)S(1)}, f32[4,1,128]{2,1,0:T(1,128)S(1)}) custom-call(f32[128,512]{1,0:T(8,128)S(1)} %copy-done.1, f32[128,256]{1,0:T(8,128)S(1)} %copy-done.2, f32[1,128]{1,0:T(1,128)S(1)} %bitcast.8, f32[256,512]{1,0:T(8,128)S(1)} %copy-done), custom_call_target="tpu_custom_call" | custom-call | tf_op jit(solution)/shard_map/pallas_call | solution.py:353
  66.1 0.0 copy-start.4
  66.1 1.6 %copy-done.4 = f32[2048,256]{1,0:T(8,128)S(1)} copy-done((f32[2048,256]{1,0:T(8,128)S(1)}, f32[2048,256]{1,0:T(8,128)}, u32[]{:S(2)}) %copy-start.4) | copy-done | bytes 2097176
  67.7 0.7 copy-done.5
  68.4 15.3 %shard_map.111 = (bf16[2048,512]{1,0:T(8,128)(2,1)S(1)}, bf16[2048,512]{1,0:T(8,128)(2,1)S(1)}, bf16[512,1024]{1,0:T(8,128)(2,1)S(1)}, bf16[512,1024]{1,0:T(8,12...) custom-call(f32[512,512]{1,0:T(8,128)S(1)} %get-tuple-element.17.w_in, ...), custom_call_target="tpu_custom_call" | custom-call | flops 4831838208 | bytes 16777216 | tf_op jit(solution)/shard_map/pallas_call | solution.py:468
  83.7 0.0 collective-permute-start.2
  83.7 1.5 %collective-permute-start.1 = (f32[8,256]{1,0:T(8,128)S(1)}, f32[8,256]{1,0:T(8,128)S(1)}, u32[]{:S(2)}, u32[]{:S(2)}) collective-permute-start(f32[8,256]{1,0:T(8,128)S(1)} %get-tuple-element.28), channel_id=1, source_target_pairs={{0,16},{8,24},{16,0},{24,8},{1,17},{9,25},{17,1},{25,9},{2,18},{10... | collective-permute-start | bytes 24584 | tf_op jit(solution)/shard_map/ppermute | solution.py:559
  85.2 0.6 collective-permute-start
  85.8 0.0 slice-done
  85.8 0.0 slice-done.1
  85.8 9.1 %shard_map.112 = f32[2048,1024]{1,0:T(8,128)} custom-call(bf16[2048,512]{1,0:T(8,128)(2,1)S(1)} %get-tuple-element.22.hi_in, bf16[2048,512]{1,0:T(8,128)(2,1)S(1)} %get-tuple-element.23.lo_in, bf16[512,1024]{1,0:T(8,128)(2,1)S(1)} %get-tuple-element.24.col_hi_in, bf16[512,1024]{1,0:T(8,128)(2,1)S(1)} %get-tuple-element.25.col_lo_in, f32[2048,1024]{1,0:T(8,128)S(1)} %bitcast.10), custom_call_target="tpu_custom_call" | custom-call | flops 6442450944 | bytes 20971520 | tf_op jit(solution)/shard_map/pallas_call | solution.py:523
  94.9 0.0 collective-permute-done.2
  94.9 0.0 collective-permute-done.1
  94.9 0.0 collective-permute-done
  94.9 0.6 fusion
  (4 shorter events, 0.0 us)
Async XLA Ops:
  0.6 1.0 %copy-start = (f32[256,512]{1,0:T(8,128)S(1)}, f32[256,512]{1,0:T(8,128)}, u32[]{:S(2)}) copy-start(f32[256,512]{1,0:T(8,128)} %panel_in.1) | copy-start | bytes 1572868
  1.7 0.9 copy-start.1
  2.6 0.9 copy-start.2
  3.5 0.7 copy-start.3
  4.2 81.6 %slice-start = ((s8[8388608]{0:T(1024)(128)(4,1)}), s8[4194304]{0:T(1024)(128)(4,1)S(1)}, s32[]{:S(2)}) async-start(s8[8388608]{0:T(1024)(128)(4,1)} %bitcast.9), calls=%async_computation | async-start | bytes 8388608
  66.1 1.6 %copy-start.4 = (f32[2048,256]{1,0:T(8,128)S(1)}, f32[2048,256]{1,0:T(8,128)}, u32[]{:S(2)}) copy-start(f32[2048,256]{1,0:T(8,128)} %geno_in.1) | copy-start | bytes 6291460
  67.7 0.7 copy-start.5
  68.4 17.5 %slice-start.1 = ((s8[8388608]{0:T(1024)(128)(4,1)}), s8[4194304]{0:T(1024)(128)(4,1)S(1)}, s32[]{:S(2)}) async-start(s8[8388608]{0:T(1024)(128)(4,1)} %bitcast.9), calls=%async_computation.1 | async-start | bytes 8388608
  83.7 11.2 %collective-permute-start.2 = (f32[8,256]{1,0:T(8,128)S(1)}, f32[8,256]{1,0:T(8,128)S(1)}, u32[]{:S(2)}, u32[]{:S(2)}) collective-permute-start(f32[8,256]{1,0:T(8,128)S(1)} %get-tuple-element.28), channel_id=1, source_target_pairs={{0,24},{8,16},{16,8},{24,0},{1,25},{9,17},{17,9},{25,1},{2,26},{10... | collective-permute-start | bytes 24584 | tf_op jit(solution)/shard_map/ppermute | solution.py:559
  83.7 11.2 %collective-permute-start.1 = (f32[8,256]{1,0:T(8,128)S(1)}, f32[8,256]{1,0:T(8,128)S(1)}, u32[]{:S(2)}, u32[]{:S(2)}) collective-permute-start(f32[8,256]{1,0:T(8,128)S(1)} %get-tuple-element.28), channel_id=1, source_target_pairs={{0,16},{8,24},{16,0},{24,8},{1,17},{9,25},{17,1},{25,9},{2,18},{10... | collective-permute-start | bytes 24584 | tf_op jit(solution)/shard_map/ppermute | solution.py:559
  85.2 9.7 %collective-permute-start = (f32[8,256]{1,0:T(8,128)S(1)}, f32[8,256]{1,0:T(8,128)S(1)}, u32[]{:S(2)}, u32[]{:S(2)}) collective-permute-start(f32[8,256]{1,0:T(8,128)S(1)} %get-tuple-element.28), channel_id=1, source_target_pairs={{0,8},{8,0},{16,24},{24,16},{1,9},{9,1},{17,25},{25,17},{2,10},{10... | collective-permute-start | bytes 24584 | tf_op jit(solution)/shard_map/ppermute | solution.py:559
where the time goes:
time: 95.8 us; the launch traced here: 95.5 us
  Pallas kernels  86.3 us (90%)
  local copies, waits for them, and re-layouts  5.83 us (6%)
  starting transfers between devices  2.14 us (2%)
    pallas_call x1, Pallas kernels, gather_and_invert(): pl.pallas_call(functools.partial(gather_kernel, ly, lz, pcol_size // prow...  61.9 us
    pallas_call x1, Pallas kernels, whiten(): pl.pallas_call(functools.partial(whiten_kernel, tile, rows_piece, col_til...  15.3 us
    pallas_call x1, Pallas kernels, update(): pl.pallas_call(update_kernel, grid=(row_count // tile,), in_specs=[left,...  9.09 us
    unnamed x16, local copies, waits for them, and re-layouts  5.83 us
    ppermute x3, starting transfers between devices, fetch(): lax.ppermute(stats, 'prow', [(i, i ^ flip) for i in range(prow_size)])  2.14 us
  transfers between devices with their start and end apart: 3, of which 0 were waited for; matrix products, arithmetic and copies ran while one was open for 0% of the time, Pallas kernels for 10%

commit v1 on v0

v1 whole, which is shorter than its diff:
```python
import functools

import jax
import jax.numpy as jnp
from jax import lax
from jax.experimental import pallas as pl
from jax.experimental.pallas import tpu as pltpu
from jax.sharding import PartitionSpec as P

MESH = pl.DeviceIdType.MESH
HIGHEST = lax.Precision.HIGHEST
TILE = 16
PARTS = 4
BLOCK = 128


def split3(value):
    hi = value.astype(jnp.bfloat16).astype(jnp.float32)
    rest = value - hi
    mid = rest.astype(jnp.bfloat16).astype(jnp.float32)
    return hi, mid, rest - mid


def tile_step(m_ref, step):
    start = pl.multiple_of(step * TILE, TILE)
    left = m_ref[pl.ds(start, TILE), :BLOCK]
    right = m_ref[pl.ds(start, TILE), BLOCK:]
    rolled = pltpu.roll(left, lax.rem(BLOCK - start, BLOCK), 1)
    cols = [jnp.broadcast_to(rolled[:, k : k + 1], (TILE, BLOCK)) for k in range(TILE)]
    rows = lax.broadcasted_iota(jnp.int32, (TILE, BLOCK), 0)
    lanes = lax.broadcasted_iota(jnp.int32, (TILE, BLOCK), 1)
    pivots = jnp.zeros_like(left)
    for j in range(TILE):
        pivot = jnp.broadcast_to(cols[j][j : j + 1, :], (TILE, BLOCK))
        inv = pl.reciprocal(pivot, approx=True)
        inv = inv * (2.0 - pivot * inv)
        below = jnp.where(rows > j, cols[j], 0.0)
        pivots = jnp.where(rows == j, pivot, pivots)

        def work(value):
            return value - below * (jnp.broadcast_to(value[j : j + 1, :], (TILE, BLOCK)) * inv)

        for k in range(j + 1, TILE):
            cols[k] = work(cols[k])
        left, right = work(left), work(right)
    scale = lax.rsqrt(pivots)
    scale = scale * (1.5 - (0.5 * pivots) * scale * scale)
    left, right = left * scale, right * scale
    m_ref[pl.ds(start, TILE), :BLOCK] = left
    m_ref[pl.ds(start, TILE), BLOCK:] = right
    both = jnp.concatenate([left, right], axis=1)
    mult = jnp.where(lanes >= start + TILE, left, 0.0)
    a0, a1, a2 = split3(mult)
    b0, b1, b2 = split3(both)
    lhs = jnp.concatenate([a0, a0, a1, a0, a1, a2], axis=0).astype(jnp.bfloat16)
    rhs = jnp.concatenate([b0, b1, b0, b2, b1, b0], axis=0).astype(jnp.bfloat16)
    m_ref[...] -= lax.dot_general(
        lhs, rhs, (((0,), (0,)), ((), ())), preferred_element_type=jnp.float32
    )


def dot_t(a, b):
    return lax.dot_general(
        a, b, (((0,), (0,)), ((), ())), precision=HIGHEST, preferred_element_type=jnp.float32
    )


def dot_n(a, b):
    return jnp.dot(a, b, precision=HIGHEST, preferred_element_type=jnp.float32)


def invert(a_ref, w_ref, m_ref, events):
    width = a_ref.shape[0]
    blocks = width // BLOCK
    tiles = BLOCK // TILE
    w_ref[...] = jnp.zeros_like(w_ref)
    eye = (
        lax.broadcasted_iota(jnp.int32, (BLOCK, BLOCK), 0)
        == lax.broadcasted_iota(jnp.int32, (BLOCK, BLOCK), 1)
    ).astype(jnp.float32)
    slot = 0
    for k in range(blocks):
        lo, hi = k * BLOCK, (k + 1) * BLOCK
        m_ref[:, :BLOCK] = a_ref[lo:hi, lo:hi]
        m_ref[:, BLOCK:] = eye
        for part in range(PARTS):

            def body(step, carry):
                tile_step(m_ref, step)
                return carry

            lax.fori_loop(part * tiles // PARTS, (part + 1) * tiles // PARTS, body, 0)
            if part < PARTS - 1:
                if slot < len(events):
                    events[slot]()
                slot += 1
        own = m_ref[:, BLOCK:]
        if k > 0:
            w_ref[lo:hi, :lo] = dot_n(own, w_ref[lo:hi, :lo])
        w_ref[lo:hi, lo:hi] = own
        if k < blocks - 1:
            upper = dot_n(own, a_ref[lo:hi, hi:])
            a_ref[hi:, hi:] -= dot_t(upper, upper)
            w_ref[hi:, :hi] -= dot_t(upper, w_ref[lo:hi, :hi])
        if slot < len(events):
            events[slot]()
        slot += 1
    while slot < len(events):
        events[slot]()
        slot += 1


LAST = ((1,), (1,))
INNER = ((1,), (0,))


def split2(value):
    hi = value.astype(jnp.bfloat16)
    return hi, (value - hi.astype(jnp.float32)).astype(jnp.bfloat16)


def dot3(a, b, dims):
    left = jnp.concatenate([a[0], a[0], a[1]], axis=dims[0][0])
    right = jnp.concatenate([b[0], b[1], b[0]], axis=dims[1][0])
    return lax.dot_general(left, right, (dims, ((), ())), preferred_element_type=jnp.float32)


def column(row):
    return jnp.transpose(jnp.broadcast_to(row, (BLOCK, row.shape[1])))


def weighted(weights, values):
    wide = jnp.concatenate([weights] * (values.shape[1] // BLOCK), axis=1)
    return jnp.sum(wide * values, axis=0, keepdims=True)


def main_kernel(
    ly, lz, group,
    diag_in, top_in, pheno_in, panel_in, trailing_in, geno_in, rest_in,
    u_out, white_out, own_out, total_out,
    a_ref, m_ref, w_ref, row_buf, col_buf, top_buf, pheno_buf, rest_buf,
    row_hi, row_lo, y_hi, y_lo, g_hi, g_lo, w_hi, w_lo, wt_hi, wt_lo, ai_hi, ai_lo,
    stat, stat_buf,
    small_send, small_recv, row_send, row_recv, col_send, col_recv, stat_send, stat_recv, local_sem,
):
    r, c = lax.axis_index("prow"), lax.axis_index("pcol")
    z, y = c // ly, lax.rem(c, ly)
    sib = r + 1 - 2 * lax.rem(r, 2)
    cross = r + 2 - 4 * (r // 2)
    diag_x = sib + 2 - 4 * (sib // 2)
    other = z * ly + (1 - y)
    rows_piece, width = panel_in.shape
    half = rows_piece // 2
    pieces = row_buf.shape[0] // rows_piece
    variants = top_in.shape[1]
    col_parts = col_buf.shape[0] // rows_piece
    root = c // group
    first = lax.rem(c, group) * col_parts
    is_root = root == r
    root_cross = root + 2 - 4 * (root // 2)
    low_end, high_end = z == 0, z == lz - 1

    barrier = pltpu.get_barrier_semaphore()

    def greet(row, col):
        pl.semaphore_signal(barrier, inc=1, device_id={"prow": row, "pcol": col}, device_id_type=MESH)

    greet(sib, c)
    greet(cross, c)
    greet(diag_x, c)
    greet(r, other)

    @pl.when(z > 0)
    def _():
        greet(r, c - ly)

    @pl.when(z < lz - 1)
    def _():
        greet(r, c + ly)

    pl.semaphore_wait(barrier, 4 + jnp.minimum(z, 1) + jnp.minimum(lz - 1 - z, 1))

    def remote(src, dst, send, recv, row, col):
        return pltpu.make_async_remote_copy(
            src_ref=src, dst_ref=dst, send_sem=send, recv_sem=recv,
            device_id={"prow": row, "pcol": col}, device_id_type=MESH,
        )

    def each(items, act):
        for item in items:
            if item[0] is True:
                act(item)
            elif item[0] is not False:
                pl.when(item[0])(functools.partial(act, item))

    def start_all(sends):
        each(sends, lambda item: item[1]().start())

    def sent_all(sends):
        each(sends, lambda item: item[1]().wait_send())

    height = diag_in.shape[0]
    side = 2 * height
    mine, theirs = (r // 2) * side, (cross // 2) * side

    def band(q):
        return pl.ds(pl.multiple_of(q * height, height), height)

    def small(kind, lane):
        part = cross if lane == 2 else r
        if kind == 0:
            if lane == 0:
                src, dst = diag_in, a_ref.at[band(r), :]
            else:
                cols = pl.ds(pl.multiple_of(theirs if lane == 2 else mine, side), side)
                dst = a_ref.at[band(part), cols]
                src = dst if lane == 2 else diag_in.at[:, cols]
        else:
            buf = (None, top_buf, pheno_buf)[kind]
            dst = buf.at[part]
            src = dst if lane == 2 else (None, top_in, pheno_in)[kind]
        return remote(
            src, dst, small_send.at[kind, lane], small_recv.at[kind, part],
            cross if lane == 1 else sib, c,
        )

    def small_wait(kind, part):
        if kind == 0:
            dst = a_ref.at[band(part), :]
            if part is not sib:
                dst = a_ref.at[band(part), pl.ds(pl.multiple_of(theirs, side), side)]
        else:
            dst = (None, top_buf, pheno_buf)[kind].at[part]
        remote(dst, dst, small_send.at[kind, 0], small_recv.at[kind, part], sib, c).wait_recv()

    def chunk(b, h):
        return row_buf.at[pl.ds(pl.multiple_of((2 * b + h) * half, half), half), :]

    def own_half(h):
        return panel_in.at[pl.ds(h * half, half), :]

    def row_copy(way, b, h, own=False):
        target = (c + ly, c - ly, other)[way]
        return lambda: remote(
            own_half(h) if own else chunk(b, h), chunk(b, h),
            row_send.at[way, 2 * b + h], row_recv.at[2 * b + h], r, target,
        )

    def row_wait(b, h):
        remote(chunk(b, h), chunk(b, h), row_send.at[0, 0], row_recv.at[2 * b + h], r, other).wait_recv()

    def col_at(i, h):
        return col_buf.at[pl.ds(pl.multiple_of((2 * i + h) * half, half), half), :]

    def col_copies(b, h, own):
        i = b - first
        src = own_half(h) if own else chunk(b, h)
        k = 2 * i + h
        return (
            remote(src, col_at(i, h), col_send.at[0, k], col_recv.at[k], cross, c),
            remote(src, col_at(i, h), col_send.at[1, k], col_recv.at[k], sib, c),
            pltpu.make_async_copy(src, col_at(i, h), local_sem.at[k]),
        )

    def col_start(b, h, own=False):
        @pl.when(is_root & (b >= first) & (b < first + col_parts))
        def _():
            for copy in col_copies(b, h, own):
                copy.start()

    def own_sends(h):
        return [
            (True, row_copy(2, c, h, True)),
            (z < lz - 1, row_copy(0, c, h, True)),
            (z > 0, row_copy(1, c, h, True)),
        ]

    def hop_arrivals(d, h):
        low, high = c - d * ly, c + d * ly
        return [
            (z >= d, low, h, [
                (z < lz - 1, row_copy(0, low, h)),
                (True if h == 0 else z != d, row_copy(2, low, h)),
            ]),
            (z + d < lz, high, h, [
                (z > 0, row_copy(1, high, h)),
                (True if h == 0 else z + d != lz - 1, row_copy(2, high, h)),
            ]),
        ]

    def across_arrivals(d, h):
        if d == 0:
            sends = []
            if h == 1 and lz > 1:
                sends = [(low_end, row_copy(0, other, h)), (high_end, row_copy(1, other, h))]
            return [(True, other, h, sends)]
        return [
            (z >= d if h == 0 else z > d, other - d * ly, h, []),
            (z + d < lz if h == 0 else z + d < lz - 1, other + d * ly, h, []),
        ]

    def far_arrivals(d):
        low, high = 1 - y, (lz - 1) * ly + 1 - y
        return [
            (z == d, low, 1, [(z < lz - 1, row_copy(0, low, 1))]),
            (z == lz - 1 - d, high, 1, [(z > 0, row_copy(1, high, 1))]),
        ]

    def arrive(items):
        def act(item):
            _, b, h, sends = item
            row_wait(b, h)
            start_all(sends)
            col_start(b, h)

        each(items, act)

    def finish(items):
        each(items, lambda item: sent_all(item[3]))

    small(0, 0).start()
    small(0, 1).start()
    diag_copy = pltpu.make_async_copy(diag_in, a_ref.at[band(r), :], local_sem.at[2 * col_parts])
    diag_copy.start()
    for h in range(2):
        start_all(own_sends(h))
    for kind in (1, 2):
        small(kind, 1).start()
        small(kind, 0).start()
    own_copies = [
        pltpu.make_async_copy(own_half(h), chunk(c, h), local_sem.at[2 * col_parts + 1 + h]) for h in range(2)
    ]
    others = [
        pltpu.make_async_copy(src, dst, local_sem.at[2 * col_parts + 3 + k])
        for k, (src, dst) in enumerate((
            (top_in, top_buf.at[r]), (pheno_in, pheno_buf.at[r]), (rest_in, rest_buf),
            (geno_in, white_out), (trailing_in, u_out),
        ))
    ]
    for copy in own_copies + others:
        copy.start()
    for h in range(2):
        col_start(c, h, True)
    small_wait(0, cross)
    small(0, 2).start()
    small_wait(0, sib)
    small_wait(0, diag_x)
    diag_copy.wait()
    small(0, 2).wait_send()

    @pl.when(r >= 2)
    def _():
        a_ref[:side, side:] = jnp.transpose(a_ref[side:, :side])

    def top_event():
        for kind in (1, 2):
            small_wait(kind, cross)
            small(kind, 2).start()

    def nothing():
        pass

    last = 2 * (lz - 1)

    def event(t):
        def run():
            if t <= last:
                arrive(hop_arrivals((t + 1) // 2, (t - 1) % 2))
            if t % 2 == 1 and t // 2 >= 1:
                arrive(far_arrivals(t // 2))
            if t == 2:
                arrive(across_arrivals(0, 0))
                arrive(across_arrivals(0, 1))
            if t >= 4 and (t - 2) // 2 < lz:
                arrive(across_arrivals((t - 2) // 2, t % 2))

        return run

    count = 2 * lz
    events = [nothing] * 16
    events[2], events[3], events[6] = event(1), top_event, event(2)
    events[10], events[14] = event(3), event(4)
    invert(a_ref, w_ref, m_ref, events)

    def prepare():
        for kind in (1, 2):
            small_wait(kind, sib)
            small_wait(kind, diag_x)
        for copy in own_copies + others:
            copy.wait()
        whole = w_ref[...]
        w_hi[...], w_lo[...] = split2(whole)
        wt_hi[...], wt_lo[...] = split2(jnp.transpose(whole))
        w, turned = (w_hi[...], w_lo[...]), (wt_hi[...], wt_lo[...])
        ai_hi[...], ai_lo[...] = split2(dot3(turned, w, INNER))
        phenos = jnp.concatenate([pheno_buf[q] for q in range(pheno_buf.shape[0])], axis=1)
        joined = jnp.concatenate([top_buf[...].reshape(width, variants), column(phenos)], axis=1)
        both = dot3(w, split2(joined), INNER)
        g_hi[...], g_lo[...] = split2(dot3(turned, split2(both), INNER))
        white = both[:, :variants]
        stat[...] = jnp.zeros_like(stat)
        stat[2:3, :] = weighted(both[:, variants:], white)
        stat[3:4, :] = jnp.sum(white * white, axis=0, keepdims=True)
        at = pl.ds(pl.multiple_of(c * rows_piece, rows_piece), rows_piece)
        own_out[...] = dot3(split2(row_buf[at, :]), (wt_hi[...], wt_lo[...]), INNER)

    unit = rest_buf.shape[2]
    units = row_buf.shape[0] // unit
    col_unit = min(col_parts, max(1, 256 // rows_piece))
    col_units = col_parts // col_unit
    col_wide = col_unit * rows_piece

    def place(b):
        return pl.ds(pl.multiple_of(b * unit, unit), unit)

    def row_step(b):
        at = place(b)
        parts = split2(row_buf[at, :])
        row_hi[at, :], row_lo[at, :] = parts
        shift = dot3(parts, (g_hi[...], g_lo[...]), INNER)
        white = white_out[at, :] - shift[:, :variants]
        white_out[at, :] = white
        stat[0:1, :] += weighted(column(rest_buf[b]) - shift[:, variants:], white)
        stat[1:2, :] += jnp.sum(white * white, axis=0, keepdims=True)

    def cols_of(q):
        return pl.ds(pl.multiple_of(q * col_wide, col_wide), col_wide)

    def block(b, q):
        at, cols = place(b), cols_of(q)
        u_out[at, cols] -= dot3((row_hi[at, :], row_lo[at, :]), (y_hi[:, cols], y_lo[:, cols]), INNER)

    def col_ready(i, h):
        @pl.when(is_root)
        def _():
            pltpu.make_async_copy(col_at(i, h), col_at(i, h), local_sem.at[2 * i + h]).wait()

        @pl.when(jnp.logical_not(is_root))
        def _():
            handed = remote(col_at(i, h), col_at(i, h), col_send.at[1, 2 * i + h], col_recv.at[2 * i + h], sib, c)
            handed.wait_recv()
            pl.when(r == root_cross)(handed.start)

    def col_step(q):
        for i in range(col_unit):
            for h in range(2):
                col_ready(q * col_unit + i, h)
        cols = cols_of(q)
        y_hi[:, cols], y_lo[:, cols] = split2(
            dot3((ai_hi[...], ai_lo[...]), split2(col_buf[cols, :]), LAST)
        )

    def over(lo, hi, fn):
        def body(k, carry):
            fn(k)
            return carry

        lax.fori_loop(lo, hi, body, 0)

    def nearest(k):
        near = jnp.minimum(z, lz - 1 - z)
        step = (k + 1) // 2
        zigzag = z + jnp.where(lax.rem(k, 2) == 1, step, -step)
        onward = jnp.where(z < lz - 1 - z, k, lz - 1 - k)
        return jnp.where(k <= 2 * near, zigzag, onward)

    def send_stats():
        stat_buf[r] = stat[...]
        for k, target in enumerate((sib, cross, diag_x)):
            remote(stat, stat_buf.at[r], stat_send.at[k], stat_recv.at[r], target, c).start()

    if lz == 4 and unit == rows_piece and col_units == 4:
        flip = (first // ly + 1 <= z)

        def row_at(k):
            own = nearest(k) * ly + y
            return own

        def col_order(q):
            zi = jnp.where(flip, 1 - q % 2, q % 2)
            yi = y if q // 2 == 0 else 1 - y
            return zi * ly + yi

        rows = [(0, 0), (0, 1), (1, 0), (2, 0), (1, 1), (3, 0), (2, 1), (3, 1)]

        def row_id(s):
            k, side_y = rows[s]
            return nearest(jnp.int32(k)) * ly + (y if side_y == 0 else 1 - y)

        def pick(values, k):
            out = values[-1]
            for j in range(len(values) - 2, -1, -1):
                out = jnp.where(k == j, values[j], out)
            return out

        row_ids = [row_id(s) for s in range(8)]
        col_ids = [col_order(q) for q in range(4)]

        def do_rows(lo, hi, done):
            def one(s):
                b = pick(row_ids, s)
                row_step(b)
                if done:
                    over(0, done, lambda q: block(b, pick(col_ids, q)))

            over(lo, hi, one)

        def do_col(q, done):
            col_step(col_ids[q])
            over(0, done, lambda s: block(pick(row_ids, s), col_ids[q]))

        prepare()
        event(5)()
        do_rows(0, 4, 0)
        do_col(0, 4)
        event(6)()
        do_rows(4, 6, 1)
        do_col(1, 6)
        arrive(across_arrivals(2, 1))
        do_rows(6, 7, 2)
        do_col(2, 7)
        arrive(far_arrivals(3))
        arrive(across_arrivals(3, 0))
        arrive(across_arrivals(3, 1))
        row_step(row_ids[7])
        send_stats()
        over(0, 3, lambda q: block(row_ids[7], pick(col_ids, q)))
        do_col(3, 8)
    else:
        for t in range(5, count + 2):
            event(t)()
        prepare()
        over(0, col_units, col_step)
        over(0, units, row_step)
        send_stats()
        over(0, units, lambda b: over(0, col_units, lambda q: block(b, q)))

    for k, source in enumerate((sib, cross, diag_x)):
        remote(stat, stat_buf.at[source], stat_send.at[k], stat_recv.at[source], sib, c).wait_recv()
    total = stat_buf[0]
    for q in range(1, stat_buf.shape[0]):
        total = total + stat_buf[q]
    people = jnp.float32(width + row_buf.shape[0] * stat_buf.shape[0])
    total_out[...] = jnp.zeros_like(total_out)
    total_out[0:1, :] = (total[0:1] + stat[2:3, :]) / jnp.sqrt(people)
    total_out[1:2, :] = (total[1:2] + stat[3:4, :]) / people

    for k in range(3):
        remote(stat, stat_buf.at[r], stat_send.at[k], stat_recv.at[r], sib, c).wait_send()
    small(0, 1).wait_send()
    small(0, 0).wait_send()
    for kind in (1, 2):
        for lane in range(3):
            small(kind, lane).wait_send()
    for h in range(2):
        sent_all(own_sends(h))
    finish(across_arrivals(0, 1))
    for d in range(1, lz):
        for h in range(2):
            finish(hop_arrivals(d, h))
        finish(far_arrivals(d))

    @pl.when(is_root)
    def _():
        def body(k, carry):
            for lane in range(2):
                remote(
                    col_at(k, 0), col_at(k, 0), col_send.at[lane, 2 * k], col_recv.at[0], sib, c
                ).wait_send()
                remote(
                    col_at(k, 1), col_at(k, 1), col_send.at[lane, 2 * k + 1], col_recv.at[0], sib, c
                ).wait_send()
            return carry

        lax.fori_loop(0, col_parts, body, 0)

    @pl.when(r == root_cross)
    def _():
        def body(k, carry):
            for h in range(2):
                remote(
                    col_at(k, h), col_at(k, h), col_send.at[1, 2 * k + h], col_recv.at[0], sib, c
                ).wait_send()
            return carry

        lax.fori_loop(0, col_parts, body, 0)


def store_kernel(u_in, white_in, own_in, total_in, u_out, white_out, own_out, score_out, info_out, sem):
    pairs = [(own_in, own_out), (white_in, white_out), (u_in, u_out)]
    pairs += [(total_in.at[0:1], score_out), (total_in.at[1:2], info_out)]
    copies = [pltpu.make_async_copy(src, dst, sem.at[k]) for k, (src, dst) in enumerate(pairs)]
    for copy in copies:
        copy.start()
    for copy in copies:
        copy.wait()


def local(diag_block, panel_cols, trailing, geno_top, geno_rest, pheno_top, pheno_rest):
    prow_size, pcol_size = lax.axis_size("prow"), lax.axis_size("pcol")
    height, width = diag_block.shape
    rows_piece = panel_cols.shape[0]
    row_count, col_count = trailing.shape
    variants = geno_top.shape[1]
    ly = 2
    lz = pcol_size // ly
    unit = min(row_count, max(rows_piece, 256))
    chunks, col_chunks = 2 * pcol_size, 2 * (col_count // rows_piece)
    f32, bf16 = jnp.float32, jnp.bfloat16
    vmem = pl.BlockSpec(memory_space=pltpu.VMEM)
    hbm = pl.BlockSpec(memory_space=pltpu.HBM)
    dma = pltpu.SemaphoreType.DMA
    wide = variants + BLOCK
    stats = (8, variants)
    arrays = [
        ((width, width), f32), ((BLOCK, 2 * BLOCK), f32), ((width, width), f32),
        ((row_count, width), f32), ((col_count, width), f32),
        ((prow_size, height, variants), f32), ((prow_size, 1, height), f32),
        ((row_count // unit, 1, unit), f32),
        ((row_count, width), bf16), ((row_count, width), bf16),
        ((width, col_count), bf16), ((width, col_count), bf16),
        ((width, wide), bf16), ((width, wide), bf16),
    ]
    arrays += [((width, width), bf16)] * 6
    arrays += [(stats, f32), ((prow_size,) + stats, f32)]
    held = pl.pallas_call(
        functools.partial(main_kernel, ly, lz, pcol_size // prow_size),
        out_shape=(
            pltpu.VMEM(trailing.shape, f32),
            pltpu.VMEM(geno_rest.shape, f32),
            pltpu.VMEM(panel_cols.shape, f32),
            pltpu.VMEM(stats, f32),
        ),
        in_specs=[hbm] * 7,
        out_specs=(vmem,) * 4,
        scratch_shapes=[pltpu.VMEM(shape, dtype) for shape, dtype in arrays]
        + [
            dma((3, 3)), dma((3, prow_size)), dma((3, chunks)), dma((chunks,)),
            dma((2, col_chunks)), dma((col_chunks,)), dma((3,)), dma((prow_size,)), dma((col_chunks + 8,)),
        ],
        compiler_params=pltpu.CompilerParams(
            collective_id=0, has_side_effects=True, vmem_limit_bytes=32 * 1024 * 1024
        ),
    )(
        *(pltpu.with_memory_space_constraint(value, pltpu.HBM) for value in (
            diag_block, geno_top, pheno_top.reshape(1, height), panel_cols, trailing, geno_rest,
            pheno_rest.reshape(row_count // unit, 1, unit),
        ))
    )
    updated_block, own_factor, white_geno, score, info = order(pl.pallas_call(
        store_kernel,
        out_shape=(
            jax.ShapeDtypeStruct(trailing.shape, f32),
            jax.ShapeDtypeStruct(geno_rest.shape, f32),
            jax.ShapeDtypeStruct(panel_cols.shape, f32),
            jax.ShapeDtypeStruct((1, variants), f32),
            jax.ShapeDtypeStruct((1, variants), f32),
        ),
        in_specs=[vmem] * 4,
        out_specs=(hbm,) * 5,
        scratch_shapes=[dma((5,))],
        compiler_params=pltpu.CompilerParams(vmem_limit_bytes=1024 * 1024),
    )(*(pltpu.with_memory_space_constraint(value, pltpu.VMEM) for value in held)))
    return (updated_block, own_factor, white_geno, score.reshape(variants), info.reshape(variants))


def order(values):
    updated, white, own, score, info = values
    return updated, own, white, score, info


def solution(mesh):
    placed = (
        P("prow", None),
        P(("prow", "pcol"), None),
        P("prow", "pcol"),
        P("prow", "pcol"),
        P("prow", "pcol"),
        P("prow"),
        P("prow"),
    )
    return jax.shard_map(
        local,
        mesh=mesh,
        in_specs=placed,
        out_specs=(
            P("prow", "pcol"),
            P(("prow", "pcol"), None),
            P("prow", "pcol"),
            P("pcol"),
            P("pcol"),
        ),
        check_vma=False,
    )
```

time: 95.8 us -> 68.9 us (0.72)
  Pallas kernels: 86.3 us -> 68 us
  local copies, waits for them, and re-layouts: 5.83 us -> 0 us
  starting transfers between devices: 2.14 us -> 0 us
    pallas_call x3 -> x2, Pallas kernels: 86.3 us -> 68 us  [the longest x1 63.6 us: local(): pl.pallas_call(functools.partial(main_kernel, ly, lz, pcol_size // prow_s...]
    unnamed x16 -> x0, local copies, waits for them, and re-layouts: 5.83 us -> none
    ppermute x3 -> x0, starting transfers between devices: 2.14 us -> none  [fetch(): lax.ppermute(stats, 'prow', [(i, i ^ flip) for i in range(prow_size)])]
  transfers between devices with their start and end apart: 3 -> 0, of which waited for: 0 -> 0; matrix products, arithmetic and copies ran while one was open for 0% -> 0% of each run, Pallas kernels for 10% -> 0%
where the time goes in v1:
time: 68.9 us; the launch traced here: 68.8 us
  Pallas kernels  68 us (99%)
  between operations  0.8 us (1%)
    pallas_call x1, Pallas kernels, local(): pl.pallas_call(functools.partial(main_kernel, ly, lz, pcol_size // prow_s...  63.6 us
    pallas_call x1, Pallas kernels, local(): pl.pallas_call(store_kernel, out_shape=(jax.ShapeDtypeStruct(trailing.sha...  4.31 us

profile of v1, /device:TPU:7, one launch (start us, length us, event | category | flops | bytes accessed | tf_op | source)
XLA Modules:
  0.0 68.8 jit_solution(14833519608653265052)
XLA Ops:
  0.6 63.6 %shard_map.110 = (f32[2048,1024]{1,0:T(8,128)S(1)}, f32[2048,256]{1,0:T(8,128)S(1)}, f32[256,512]{1,0:T(8,128)S(1)}, f32[8,256]{1,0:T(8,128)S(1)}) custom-call(f32[128,512]{1,0:T(8,128)} %diag_in.1, f32[128,256]{1,0:T(8,128)} %top_in.1, f32[1,128]{1,0:T(1,128)} %bitcast.5, f32[256,512]{1,0:T(8,128)} %panel_in.1, f32[2048,1024]{1,0:T(8,128)} %trailing_in.1, ...), custom_call_target="tpu_custom_call" | custom-call | tf_op jit(solution)/shard_map/pallas_call | solution.py:626
  64.3 4.3 %shard_map.111 = (f32[2048,1024]{1,0:T(8,128)}, f32[2048,256]{1,0:T(8,128)}, f32[256,512]{1,0:T(8,128)}, f32[1,256]{1,0:T(1,128)}, f32[1,256]{1,0:T(1,128)}) custom-call(f32[2048,1024]{1,0:T(8,128)S(1)} %get-tuple-element.14.u_in, f32[2048,256]{1,0:T(8,128)S(1)} %get-tuple-element.15.white_in, f32[256,512]{1,0:T(8,128)S(1)} %get-tuple-element.16.own_in, ...), custom_call_target="tpu_custom_call" | custom-call | tf_op jit(solution)/shard_map/pallas_call | solution.py:650

commit v2 on v1

--- a/solution.py
+++ b/solution.py
@@ -23,26 +23,55 @@
 
 def tile_step(m_ref, step):
     start = pl.multiple_of(step * TILE, TILE)
+    half = TILE // 2
     left = m_ref[pl.ds(start, TILE), :BLOCK]
     right = m_ref[pl.ds(start, TILE), BLOCK:]
     rolled = pltpu.roll(left, lax.rem(BLOCK - start, BLOCK), 1)
-    cols = [jnp.broadcast_to(rolled[:, k : k + 1], (TILE, BLOCK)) for k in range(TILE)]
-    rows = lax.broadcasted_iota(jnp.int32, (TILE, BLOCK), 0)
+    rows = lax.broadcasted_iota(jnp.int32, (half, BLOCK), 0)
     lanes = lax.broadcasted_iota(jnp.int32, (TILE, BLOCK), 1)
-    pivots = jnp.zeros_like(left)
-    for j in range(TILE):
-        pivot = jnp.broadcast_to(cols[j][j : j + 1, :], (TILE, BLOCK))
-        inv = pl.reciprocal(pivot, approx=True)
-        inv = inv * (2.0 - pivot * inv)
-        below = jnp.where(rows > j, cols[j], 0.0)
-        pivots = jnp.where(rows == j, pivot, pivots)
-
-        def work(value):
-            return value - below * (jnp.broadcast_to(value[j : j + 1, :], (TILE, BLOCK)) * inv)
-
-        for k in range(j + 1, TILE):
-            cols[k] = work(cols[k])
-        left, right = work(left), work(right)
+
+    def halves(value):
+        return [value[:half], value[half:]]
+
+    def spread(parts, j):
+        part, at = parts[j // half], j % half
+        return jnp.broadcast_to(part[at : at + 1, :], (half, BLOCK))
+
+    cols = [halves(jnp.broadcast_to(rolled[:, k : k + 1], (TILE, BLOCK))) for k in range(TILE)]
+    values = [halves(left), halves(right)]
+    pivots = [jnp.zeros((half, BLOCK), jnp.float32) for _ in range(2)]
+    def inverse(value):
+        inv = pl.reciprocal(value, approx=True)
+        return inv * (2.0 - value * inv)
+
+    for j in range(0, TILE, 2):
+        own, low = j // half, j % half
+        one, two = cols[j], cols[j + 1]
+        p, b, c = spread(one, j), spread(one, j + 1), spread(two, j + 1)
+        det = p * c - b * b
+        inv_p, inv_det = inverse(p), inverse(det)
+        ratio = b * inv_p
+        pivots[own] = jnp.where(rows == low, p, jnp.where(rows == low + 1, det * inv_p, pivots[own]))
+        lead, tail, after = {}, {}, [None, None]
+        for part in range(own, 2):
+            after[part] = two[part] - ratio * one[part]
+            lead[part] = one[part] * inv_p
+            tail[part] = (p * two[part] - b * one[part]) * inv_det
+            if part == own:
+                lead[part] = jnp.where(rows > low, lead[part], 0.0)
+                tail[part] = jnp.where(rows > low + 1, tail[part], 0.0)
+        for k in range(j + 2, TILE):
+            top, under = spread(one, k), spread(after, k)
+            for part in lead:
+                if part >= k // half:
+                    cols[k][part] = (cols[k][part] - lead[part] * top) - tail[part] * under
+        for value in values:
+            top = spread(value, j)
+            under = spread(value, j + 1) - ratio * top
+            for part in lead:
+                value[part] = (value[part] - lead[part] * top) - tail[part] * under
+    left, right = (jnp.concatenate(value, axis=0) for value in values)
+    pivots = jnp.concatenate(pivots, axis=0)
     scale = lax.rsqrt(pivots)
     scale = scale * (1.5 - (0.5 * pivots) * scale * scale)
     left, right = left * scale, right * scale
@@ -132,6 +161,72 @@
 def weighted(weights, values):
     wide = jnp.concatenate([weights] * (values.shape[1] // BLOCK), axis=1)
     return jnp.sum(wide * values, axis=0, keepdims=True)
+
+
+def orders(ly, lz, first, z, y):
+    low_end, high_end = z == 0, z == lz - 1
+    far = (low_end & (y == 1)) | (high_end & (y == 0))
+
+    def nearest(k):
+        near = jnp.minimum(z, lz - 1 - z)
+        step = (k + 1) // 2
+        zigzag = z + (step if k % 2 == 1 else -step)
+        onward = jnp.where(z < lz - 1 - z, k, lz - 1 - k)
+        return jnp.where(k <= 2 * near, zigzag, onward)
+
+    def row(k, turned):
+        return nearest(k) * ly + (1 - y if turned else y)
+
+    row_ids = [
+        row(0, False), row(0, True), row(1, False), row(2, False),
+        row(1, True), row(3, False), row(2, True), row(3, True),
+    ]
+    flip = first // ly + 1 <= z
+    col_ids = [
+        jnp.where(flip, 1 - q % 2, q % 2) * ly + (y if q // 2 == 0 else 1 - y) for q in range(4)
+    ]
+    return far, row_ids, col_ids
+
+
+def pick(values, k):
+    out = values[-1]
+    for j in range(len(values) - 2, -1, -1):
+        out = jnp.where(k == j, values[j], out)
+    return out
+
+
+def over(lo, hi, fn):
+    def body(k, carry):
+        fn(k)
+        return carry
+
+    lax.fori_loop(lo, hi, body, 0)
+
+
+def is_tuned(lz, rows_piece, col_parts):
+    return lz == 4 and rows_piece == 256 and col_parts == 4
+
+
+def grid_copies(tuned, far_side, near_side, row_ids, col_ids, rows_piece, outward, sem):
+    if not tuned:
+        src, dst = (near_side, far_side) if outward else (far_side, near_side)
+        pltpu.make_async_copy(src, dst, sem).start()
+        return
+
+    def one(k):
+        i, j = k // 4, lax.rem(k, 4)
+
+        def at(ref, row, col):
+            return ref.at[
+                pl.ds(pl.multiple_of(row * rows_piece, rows_piece), rows_piece),
+                pl.ds(pl.multiple_of(col * rows_piece, rows_piece), rows_piece),
+            ]
+
+        here, there = at(near_side, i, j), at(far_side, pick(row_ids, i), pick(col_ids, j))
+        src, dst = (here, there) if outward else (there, here)
+        pltpu.make_async_copy(src, dst, sem).start()
+
+    over(0, 32, one)
 
 
 def main_kernel(
@@ -159,6 +254,8 @@
     is_root = root == r
     root_cross = root + 2 - 4 * (root // 2)
     low_end, high_end = z == 0, z == lz - 1
+    tuned = is_tuned(lz, rows_piece, col_parts)
+    far, row_ids, col_ids = orders(ly, lz, first, z, y) if tuned else (None, None, None)
 
     barrier = pltpu.get_barrier_semaphore()
 
@@ -277,15 +374,11 @@
 
     def hop_arrivals(d, h):
         low, high = c - d * ly, c + d * ly
+        low_over = True if h == 0 else z != d
+        high_over = True if h == 0 else z + d != lz - 1
         return [
-            (z >= d, low, h, [
-                (z < lz - 1, row_copy(0, low, h)),
-                (True if h == 0 else z != d, row_copy(2, low, h)),
-            ]),
-            (z + d < lz, high, h, [
-                (z > 0, row_copy(1, high, h)),
-                (True if h == 0 else z + d != lz - 1, row_copy(2, high, h)),
-            ]),
+            (z >= d, low, h, [(z < lz - 1, row_copy(0, low, h)), (low_over, row_copy(2, low, h))]),
+            (z + d < lz, high, h, [(z > 0, row_copy(1, high, h)), (high_over, row_copy(2, high, h))]),
         ]
 
     def across_arrivals(d, h):
@@ -334,13 +427,16 @@
         pltpu.make_async_copy(src, dst, local_sem.at[2 * col_parts + 3 + k])
         for k, (src, dst) in enumerate((
             (top_in, top_buf.at[r]), (pheno_in, pheno_buf.at[r]), (rest_in, rest_buf),
-            (geno_in, white_out), (trailing_in, u_out),
+            (geno_in, white_out),
         ))
     ]
     for copy in own_copies + others:
         copy.start()
     for h in range(2):
         col_start(c, h, True)
+    trailing_sem = local_sem.at[2 * col_parts + 7]
+    grid_copies(tuned, trailing_in, u_out, row_ids, col_ids, rows_piece, False, trailing_sem)
+    others.append(pltpu.make_async_copy(trailing_in, u_out, trailing_sem))
     small_wait(0, cross)
     small(0, 2).start()
     small_wait(0, sib)
@@ -379,7 +475,7 @@
     count = 2 * lz
     events = [nothing] * 16
     events[2], events[3], events[6] = event(1), top_event, event(2)
-    events[10], events[14] = event(3), event(4)
+    events[11], events[15] = event(3), event(4)
     invert(a_ref, w_ref, m_ref, events)
 
     def prepare():
@@ -413,22 +509,23 @@
     def place(b):
         return pl.ds(pl.multiple_of(b * unit, unit), unit)
 
-    def row_step(b):
-        at = place(b)
+    def row_step(k, b):
+        at, slot = place(b), place(k)
         parts = split2(row_buf[at, :])
-        row_hi[at, :], row_lo[at, :] = parts
+        row_hi[slot, :], row_lo[slot, :] = parts
         shift = dot3(parts, (g_hi[...], g_lo[...]), INNER)
         white = white_out[at, :] - shift[:, :variants]
         white_out[at, :] = white
         stat[0:1, :] += weighted(column(rest_buf[b]) - shift[:, variants:], white)
         stat[1:2, :] += jnp.sum(white * white, axis=0, keepdims=True)
 
-    def cols_of(q):
-        return pl.ds(pl.multiple_of(q * col_wide, col_wide), col_wide)
-
-    def block(b, q):
-        at, cols = place(b), cols_of(q)
-        u_out[at, cols] -= dot3((row_hi[at, :], row_lo[at, :]), (y_hi[:, cols], y_lo[:, cols]), INNER)
+    def cols_of(q, count=1):
+        return pl.ds(pl.multiple_of(q * col_wide, col_wide), col_wide * count)
+
+    def product(k, many, q, count):
+        slots = pl.ds(pl.multiple_of(k * unit, unit), unit * many)
+        cols = cols_of(q, count)
+        return dot3((row_hi[slots, :], row_lo[slots, :]), (y_hi[:, cols], y_lo[:, cols]), INNER)
 
     def col_ready(i, h):
         @pl.when(is_root)
@@ -441,99 +538,85 @@
             handed.wait_recv()
             pl.when(r == root_cross)(handed.start)
 
-    def col_step(q):
+    def cols_ready(unit_at):
         for i in range(col_unit):
             for h in range(2):
-                col_ready(q * col_unit + i, h)
-        cols = cols_of(q)
-        y_hi[:, cols], y_lo[:, cols] = split2(
-            dot3((ai_hi[...], ai_lo[...]), split2(col_buf[cols, :]), LAST)
+                col_ready(unit_at * col_unit + i, h)
+
+    def col_step(q, unit_at, waits=True):
+        if waits:
+            cols_ready(unit_at)
+        y_hi[:, cols_of(q)], y_lo[:, cols_of(q)] = split2(
+            dot3((ai_hi[...], ai_lo[...]), split2(col_buf[cols_of(unit_at), :]), LAST)
         )
-
-    def over(lo, hi, fn):
-        def body(k, carry):
-            fn(k)
-            return carry
-
-        lax.fori_loop(lo, hi, body, 0)
-
-    def nearest(k):
-        near = jnp.minimum(z, lz - 1 - z)
-        step = (k + 1) // 2
-        zigzag = z + jnp.where(lax.rem(k, 2) == 1, step, -step)
-        onward = jnp.where(z < lz - 1 - z, k, lz - 1 - k)
-        return jnp.where(k <= 2 * near, zigzag, onward)
 
     def send_stats():
         stat_buf[r] = stat[...]
         for k, target in enumerate((sib, cross, diag_x)):
             remote(stat, stat_buf.at[r], stat_send.at[k], stat_recv.at[r], target, c).start()
 
-    if lz == 4 and unit == rows_piece and col_units == 4:
-        flip = (first // ly + 1 <= z)
-
-        def row_at(k):
-            own = nearest(k) * ly + y
-            return own
-
-        def col_order(q):
-            zi = jnp.where(flip, 1 - q % 2, q % 2)
-            yi = y if q // 2 == 0 else 1 - y
-            return zi * ly + yi
-
-        rows = [(0, 0), (0, 1), (1, 0), (2, 0), (1, 1), (3, 0), (2, 1), (3, 1)]
-
-        def row_id(s):
-            k, side_y = rows[s]
-            return nearest(jnp.int32(k)) * ly + (y if side_y == 0 else 1 - y)
-
-        def pick(values, k):
-            out = values[-1]
-            for j in range(len(values) - 2, -1, -1):
-                out = jnp.where(k == j, values[j], out)
-            return out
-
-        row_ids = [row_id(s) for s in range(8)]
-        col_ids = [col_order(q) for q in range(4)]
-
-        def do_rows(lo, hi, done):
-            def one(s):
-                b = pick(row_ids, s)
-                row_step(b)
-                if done:
-                    over(0, done, lambda q: block(b, pick(col_ids, q)))
-
-            over(lo, hi, one)
-
-        def do_col(q, done):
-            col_step(col_ids[q])
-            over(0, done, lambda s: block(pick(row_ids, s), col_ids[q]))
+    if tuned:
+        near = jnp.logical_not(far)
+
+        def apply(k, many, q, count):
+            u_out[pl.ds(pl.multiple_of(k * unit, unit), unit * many), cols_of(q, count)] -= product(k, many, q, count)
+
+        def first_stage():
+            arrive(across_arrivals(1, 1))
+            arrive(hop_arrivals(3, 0))
+            arrive(far_arrivals(2))
+
+        def second_stage():
+            arrive(across_arrivals(2, 0))
+            arrive(hop_arrivals(3, 1))
+            arrive(across_arrivals(2, 1))
+
+        def stage(t):
+            pl.when(t == 0)(first_stage)
+            pl.when(t == 1)(second_stage)
+            pl.when(t < 3)(lambda: row_step(4 + t, pick(row_ids, 4 + t)))
+
+            @pl.when((t < 3) | near)
+            def _():
+                col_step(t, pick(col_ids, t))
+                apply(0, 4, t, 1)
+
+        def last_rows():
+            arrive(far_arrivals(3))
+            arrive(across_arrivals(3, 0))
+            row_step(7, row_ids[7])
+            send_stats()
+
+        def rest(k):
+            pl.when((k == 6) & far)(lambda: cols_ready(col_ids[3]))
+            pl.when(near)(lambda: apply(k, 1, 0, 4))
+            pl.when(far)(lambda: apply(k, 1, 0, 3))
 
         prepare()
-        event(5)()
-        do_rows(0, 4, 0)
-        do_col(0, 4)
-        event(6)()
-        do_rows(4, 6, 1)
-        do_col(1, 6)
-        arrive(across_arrivals(2, 1))
-        do_rows(6, 7, 2)
-        do_col(2, 7)
-        arrive(far_arrivals(3))
-        arrive(across_arrivals(3, 0))
-        arrive(across_arrivals(3, 1))
-        row_step(row_ids[7])
-        send_stats()
-        over(0, 3, lambda q: block(row_ids[7], pick(col_ids, q)))
-        do_col(3, 8)
+        over(0, 4, lambda k: row_step(k, pick(row_ids, k)))
+        over(0, 4, stage)
+        last_rows()
+        over(4, 8, rest)
+
+        @pl.when(far)
+        def _():
+            col_step(3, col_ids[3], False)
+            over(0, 2, lambda g: apply(4 * g, 4, 3, 1))
     else:
         for t in range(5, count + 2):
             event(t)()
         prepare()
-        over(0, col_units, col_step)
-        over(0, units, row_step)
+
+        def apply(k):
+            over(0, col_units, lambda q: apply_one(k, q))
+
+        def apply_one(k, q):
+            u_out[place(k), cols_of(q)] -= product(k, 1, q, 1)
+
+        over(0, col_units, lambda q: col_step(q, q))
+        over(0, units, lambda k: row_step(k, k))
         send_stats()
-        over(0, units, lambda b: over(0, col_units, lambda q: block(b, q)))
+        over(0, units, apply)
 
     for k, source in enumerate((sib, cross, diag_x)):
         remote(stat, stat_buf.at[source], stat_send.at[k], stat_recv.at[source], sib, c).wait_recv()
@@ -586,14 +669,23 @@
         lax.fori_loop(0, col_parts, body, 0)
 
 
-def store_kernel(u_in, white_in, own_in, total_in, u_out, white_out, own_out, score_out, info_out, sem):
-    pairs = [(own_in, own_out), (white_in, white_out), (u_in, u_out)]
+def store_kernel(ly, lz, group, u_in, white_in, own_in, total_in, u_out, white_out, own_out, score_out, info_out, sem):
+    c = lax.axis_index("pcol")
+    rows_piece = own_in.shape[0]
+    col_parts = u_in.shape[1] // rows_piece
+    tuned = is_tuned(lz, rows_piece, col_parts)
+    row_ids, col_ids = None, None
+    if tuned:
+        _, row_ids, col_ids = orders(ly, lz, lax.rem(c, group) * col_parts, c // ly, lax.rem(c, ly))
+    grid_copies(tuned, u_out, u_in, row_ids, col_ids, rows_piece, True, sem.at[0])
+    pairs = [(own_in, own_out), (white_in, white_out)]
     pairs += [(total_in.at[0:1], score_out), (total_in.at[1:2], info_out)]
-    copies = [pltpu.make_async_copy(src, dst, sem.at[k]) for k, (src, dst) in enumerate(pairs)]
+    copies = [pltpu.make_async_copy(src, dst, sem.at[1 + k]) for k, (src, dst) in enumerate(pairs)]
     for copy in copies:
         copy.start()
     for copy in copies:
         copy.wait()
+    pltpu.make_async_copy(u_in, u_out, sem.at[0]).wait()
 
 
 def local(diag_block, panel_cols, trailing, geno_top, geno_rest, pheno_top, pheno_rest):
@@ -636,7 +728,7 @@
         scratch_shapes=[pltpu.VMEM(shape, dtype) for shape, dtype in arrays]
         + [
             dma((3, 3)), dma((3, prow_size)), dma((3, chunks)), dma((chunks,)),
-            dma((2, col_chunks)), dma((col_chunks,)), dma((3,)), dma((prow_size,)), dma((col_chunks + 8,)),
+            dma((2, col_chunks)), dma((col_chunks,)), dma((3,)), dma((prow_size,)), dma((col_chunks + 9,)),
         ],
         compiler_params=pltpu.CompilerParams(
             collective_id=0, has_side_effects=True, vmem_limit_bytes=32 * 1024 * 1024
@@ -648,7 +740,7 @@
         ))
     )
     updated_block, own_factor, white_geno, score, info = order(pl.pallas_call(
-        store_kernel,
+        functools.partial(store_kernel, ly, lz, pcol_size // prow_size),
         out_shape=(
             jax.ShapeDtypeStruct(trailing.shape, f32),
             jax.ShapeDtypeStruct(geno_rest.shape, f32),

time: 68.9 us -> 66.8 us (0.970)
  Pallas kernels: 68 us -> 65.8 us
    pallas_call x1, Pallas kernels: 63.6 us -> 61.6 us  [local(): pl.pallas_call(functools.partial(main_kernel, ly, lz, pcol_size // prow_s...]
where the time goes in v2:
time: 66.8 us; the launch traced here: 66.6 us
  Pallas kernels  65.8 us (99%)
  between operations  0.8 us (1%)
    pallas_call x1, Pallas kernels, local(): pl.pallas_call(functools.partial(main_kernel, ly, lz, pcol_size // prow_s...  61.6 us
    pallas_call x1, Pallas kernels, local(): pl.pallas_call(functools.partial(store_kernel, ly, lz, pcol_size // prow_...  4.21 us

profile of v2, /device:TPU:7, one launch (start us, length us, event | category | flops | bytes accessed | tf_op | source)
XLA Modules:
  0.0 66.6 jit_solution(14826329270861502115)
XLA Ops:
  0.6 61.6 %shard_map.110 = (f32[2048,1024]{1,0:T(8,128)S(1)}, f32[2048,256]{1,0:T(8,128)S(1)}, f32[256,512]{1,0:T(8,128)S(1)}, f32[8,256]{1,0:T(8,128)S(1)}) custom-call(f32[128,512]{1,0:T(8,128)} %diag_in.1, f32[128,256]{1,0:T(8,128)} %top_in.1, f32[1,128]{1,0:T(1,128)} %bitcast.5, f32[256,512]{1,0:T(8,128)} %panel_in.1, f32[2048,1024]{1,0:T(8,128)} %trailing_in.1, ...), custom_call_target="tpu_custom_call" | custom-call | tf_op jit(solution)/shard_map/pallas_call | solution.py:718
  62.2 4.2 %shard_map.111 = (f32[2048,1024]{1,0:T(8,128)}, f32[2048,256]{1,0:T(8,128)}, f32[256,512]{1,0:T(8,128)}, f32[1,256]{1,0:T(1,128)}, f32[1,256]{1,0:T(1,128)}) custom-call(f32[2048,1024]{1,0:T(8,128)S(1)} %get-tuple-element.14.u_in, f32[2048,256]{1,0:T(8,128)S(1)} %get-tuple-element.15.white_in, f32[256,512]{1,0:T(8,128)S(1)} %get-tuple-element.16.own_in, ...), custom_call_target="tpu_custom_call" | custom-call | tf_op jit(solution)/shard_map/pallas_call | solution.py:742

commit v3 on v2

--- a/solution.py
+++ b/solution.py
@@ -10,6 +10,7 @@
 MESH = pl.DeviceIdType.MESH
 HIGHEST = lax.Precision.HIGHEST
 TILE = 16
+FINE = 4
 PARTS = 4
 BLOCK = 128
 
@@ -237,6 +238,7 @@
     row_hi, row_lo, y_hi, y_lo, g_hi, g_lo, w_hi, w_lo, wt_hi, wt_lo, ai_hi, ai_lo,
     stat, stat_buf,
     small_send, small_recv, row_send, row_recv, col_send, col_recv, stat_send, stat_recv, local_sem,
+    fine_send, fine_recv, fine_col_send, fine_col_recv, fine_local,
 ):
     r, c = lax.axis_index("prow"), lax.axis_index("pcol")
     z, y = c // ly, lax.rem(c, ly)
@@ -303,13 +305,16 @@
     def band(q):
         return pl.ds(pl.multiple_of(q * height, height), height)
 
+    def half_cols(start, kind):
+        return pl.ds(pl.multiple_of(start + (height if kind == 3 else 0), height), height)
+
     def small(kind, lane):
         part = cross if lane == 2 else r
-        if kind == 0:
+        if kind in (0, 3):
             if lane == 0:
                 src, dst = diag_in, a_ref.at[band(r), :]
             else:
-                cols = pl.ds(pl.multiple_of(theirs if lane == 2 else mine, side), side)
+                cols = half_cols(theirs if lane == 2 else mine, kind)
                 dst = a_ref.at[band(part), cols]
                 src = dst if lane == 2 else diag_in.at[:, cols]
         else:
@@ -322,10 +327,10 @@
         )
 
     def small_wait(kind, part):
-        if kind == 0:
+        if kind in (0, 3):
             dst = a_ref.at[band(part), :]
             if part is not sib:
-                dst = a_ref.at[band(part), pl.ds(pl.multiple_of(theirs, side), side)]
+                dst = a_ref.at[band(part), half_cols(theirs, kind)]
         else:
             dst = (None, top_buf, pheno_buf)[kind].at[part]
         remote(dst, dst, small_send.at[kind, 0], small_recv.at[kind, part], sib, c).wait_recv()
@@ -365,6 +370,76 @@
             for copy in col_copies(b, h, own):
                 copy.start()
 
+    def part(ref, b, h, p):
+        rows = half // FINE
+        return ref.at[pl.ds(pl.multiple_of((2 * b + h) * half + p * rows, rows), rows), :]
+
+    def fine_copies(way, b, h):
+        target = (c + ly, c - ly, other)[way]
+
+        def one(p):
+            return lambda: remote(
+                part(row_buf, b, h, p), part(row_buf, b, h, p), fine_send.at[h, p], fine_recv.at[h, p], r, target
+            )
+
+        return [one(p) for p in range(FINE)]
+
+    last_piece = jnp.where(low_end, (lz - 1) * ly, 0) + 1 - y
+
+    def fine_col(h, p):
+        src, dst = part(row_buf, last_piece, h, p), part(col_buf, last_piece - first, h, p)
+        return (
+            remote(src, dst, fine_col_send.at[0, h, p], fine_col_recv.at[h, p], cross, c),
+            remote(src, dst, fine_col_send.at[1, h, p], fine_col_recv.at[h, p], sib, c),
+            pltpu.make_async_copy(src, dst, fine_local.at[h, p]),
+        )
+
+    def fine_handed(h, p):
+        dst = part(col_buf, last_piece - first, h, p)
+        return remote(dst, dst, fine_col_send.at[1, h, p], fine_col_recv.at[h, p], sib, c)
+
+    def fine_arrive():
+        for p in range(FINE):
+            for h in (1, 0):
+                dst = part(row_buf, last_piece, h, p)
+                remote(dst, dst, fine_send.at[h, p], fine_recv.at[h, p], r, other).wait_recv()
+
+                @pl.when(is_root & far)
+                def _():
+                    for copy in fine_col(h, p):
+                        copy.start()
+
+    def fine_hand():
+        for p in range(FINE):
+            for h in (1, 0):
+                fine_handed(h, p).wait_recv()
+                fine_handed(h, p).start()
+
+    def fine_ready():
+        for p in range(FINE):
+            for h in (1, 0):
+
+                @pl.when(is_root)
+                def _():
+                    fine_col(h, p)[2].wait()
+
+                @pl.when(jnp.logical_not(is_root) & (r != root_cross))
+                def _():
+                    fine_handed(h, p).wait_recv()
+
+    def fine_sent():
+        for p in range(FINE):
+            for h in (1, 0):
+
+                @pl.when(is_root)
+                def _():
+                    for copy in fine_col(h, p)[:2]:
+                        copy.wait_send()
+
+                @pl.when(r == root_cross)
+                def _():
+                    fine_handed(h, p).wait_send()
+
     def own_sends(h):
         return [
             (True, row_copy(2, c, h, True)),
@@ -376,9 +451,13 @@
         low, high = c - d * ly, c + d * ly
         low_over = True if h == 0 else z != d
         high_over = True if h == 0 else z + d != lz - 1
+        low_across, high_across = [(low_over, row_copy(2, low, h))], [(high_over, row_copy(2, high, h))]
+        if tuned and d == lz - 1 and h == 0:
+            low_across = [(True, copy) for copy in fine_copies(2, low, h)]
+            high_across = [(True, copy) for copy in fine_copies(2, high, h)]
         return [
-            (z >= d, low, h, [(z < lz - 1, row_copy(0, low, h)), (low_over, row_copy(2, low, h))]),
-            (z + d < lz, high, h, [(z > 0, row_copy(1, high, h)), (high_over, row_copy(2, high, h))]),
+            (z >= d, low, h, [(z < lz - 1, row_copy(0, low, h))] + low_across),
+            (z + d < lz, high, h, [(z > 0, row_copy(1, high, h))] + high_across),
         ]
 
     def across_arrivals(d, h):
@@ -394,9 +473,12 @@
 
     def far_arrivals(d):
         low, high = 1 - y, (lz - 1) * ly + 1 - y
+        ups, downs = [row_copy(0, low, 1)], [row_copy(1, high, 1)]
+        if tuned and d == lz - 2:
+            ups, downs = fine_copies(0, low, 1), fine_copies(1, high, 1)
         return [
-            (z == d, low, 1, [(z < lz - 1, row_copy(0, low, 1))]),
-            (z == lz - 1 - d, high, 1, [(z > 0, row_copy(1, high, 1))]),
+            (z == d, low, 1, [(z < lz - 1, copy) for copy in ups]),
+            (z == lz - 1 - d, high, 1, [(z > 0, copy) for copy in downs]),
         ]
 
     def arrive(items):
@@ -411,8 +493,9 @@
     def finish(items):
         each(items, lambda item: sent_all(item[3]))
 
+    small(0, 1).start()
     small(0, 0).start()
-    small(0, 1).start()
+    small(3, 1).start()
     diag_copy = pltpu.make_async_copy(diag_in, a_ref.at[band(r), :], local_sem.at[2 * col_parts])
     diag_copy.start()
     for h in range(2):
@@ -442,11 +525,19 @@
     small_wait(0, sib)
     small_wait(0, diag_x)
     diag_copy.wait()
-    small(0, 2).wait_send()
-
-    @pl.when(r >= 2)
-    def _():
-        a_ref[:side, side:] = jnp.transpose(a_ref[side:, :side])
+
+    def diag_event():
+        small_wait(3, cross)
+        small(3, 2).start()
+
+    def corner_event():
+        small_wait(3, diag_x)
+        small(0, 2).wait_send()
+        small(3, 2).wait_send()
+
+        @pl.when(r >= 2)
+        def _():
+            a_ref[:side, side:] = jnp.transpose(a_ref[side:, :side])
 
     def top_event():
         for kind in (1, 2):
@@ -474,7 +565,8 @@
 
     count = 2 * lz
     events = [nothing] * 16
-    events[2], events[3], events[6] = event(1), top_event, event(2)
+    events[0], events[2], events[3] = diag_event, corner_event, event(1)
+    events[4], events[7] = top_event, event(2)
     events[11], events[15] = event(3), event(4)
     invert(a_ref, w_ref, m_ref, events)
 
@@ -561,13 +653,17 @@
         def apply(k, many, q, count):
             u_out[pl.ds(pl.multiple_of(k * unit, unit), unit * many), cols_of(q, count)] -= product(k, many, q, count)
 
+        def only(cond, items):
+            return [(cond if item[0] is True else item[0] & cond,) + tuple(item[1:]) for item in items]
+
         def first_stage():
             arrive(across_arrivals(1, 1))
             arrive(hop_arrivals(3, 0))
             arrive(far_arrivals(2))
+            arrive(only(low_end | high_end, across_arrivals(2, 0)))
 
         def second_stage():
-            arrive(across_arrivals(2, 0))
+            arrive(only((z > 0) & (z < lz - 1), across_arrivals(2, 0)))
             arrive(hop_arrivals(3, 1))
             arrive(across_arrivals(2, 1))
 
@@ -576,21 +672,20 @@
             pl.when(t == 1)(second_stage)
             pl.when(t < 3)(lambda: row_step(4 + t, pick(row_ids, 4 + t)))
 
-            @pl.when((t < 3) | near)
+            @pl.when((t < 2) | near)
             def _():
                 col_step(t, pick(col_ids, t))
                 apply(0, 4, t, 1)
 
         def last_rows():
-            arrive(far_arrivals(3))
-            arrive(across_arrivals(3, 0))
+            pl.when(low_end | high_end)(fine_arrive)
             row_step(7, row_ids[7])
             send_stats()
 
         def rest(k):
-            pl.when((k == 6) & far)(lambda: cols_ready(col_ids[3]))
+            pl.when((k == 5) & far)(lambda: cols_ready(col_ids[2]))
             pl.when(near)(lambda: apply(k, 1, 0, 4))
-            pl.when(far)(lambda: apply(k, 1, 0, 3))
+            pl.when(far)(lambda: apply(k, 1, 0, 2))
 
         prepare()
         over(0, 4, lambda k: row_step(k, pick(row_ids, k)))
@@ -598,10 +693,17 @@
         last_rows()
         over(4, 8, rest)
 
-        @pl.when(far)
-        def _():
-            col_step(3, col_ids[3], False)
-            over(0, 2, lambda g: apply(4 * g, 4, 3, 1))
+        def late_column(t):
+            pl.when(t == 3)(fine_ready)
+            col_step(t, pick(col_ids, t), False)
+
+            def part_of_rows(g):
+                pl.when((t == 2) & (g == 1) & (r == root_cross))(fine_hand)
+                apply(4 * g, 4, t, 1)
+
+            over(0, 2, part_of_rows)
+
+        pl.when(far)(lambda: over(2, 4, late_column))
     else:
         for t in range(5, count + 2):
             event(t)()
@@ -630,8 +732,9 @@
 
     for k in range(3):
         remote(stat, stat_buf.at[r], stat_send.at[k], stat_recv.at[r], sib, c).wait_send()
-    small(0, 1).wait_send()
-    small(0, 0).wait_send()
+    for lane in range(2):
+        small(0, lane).wait_send()
+    small(3, 1).wait_send()
     for kind in (1, 2):
         for lane in range(3):
             small(kind, lane).wait_send()
@@ -643,30 +746,25 @@
             finish(hop_arrivals(d, h))
         finish(far_arrivals(d))
 
-    @pl.when(is_root)
-    def _():
-        def body(k, carry):
-            for lane in range(2):
-                remote(
-                    col_at(k, 0), col_at(k, 0), col_send.at[lane, 2 * k], col_recv.at[0], sib, c
-                ).wait_send()
-                remote(
-                    col_at(k, 1), col_at(k, 1), col_send.at[lane, 2 * k + 1], col_recv.at[0], sib, c
-                ).wait_send()
-            return carry
-
-        lax.fori_loop(0, col_parts, body, 0)
-
-    @pl.when(r == root_cross)
-    def _():
-        def body(k, carry):
+    skip = jnp.where(far, last_piece - first, col_parts) if tuned else col_parts
+
+    def sent(k):
+        def act():
             for h in range(2):
-                remote(
+                handed = remote(
                     col_at(k, h), col_at(k, h), col_send.at[1, 2 * k + h], col_recv.at[0], sib, c
-                ).wait_send()
-            return carry
-
-        lax.fori_loop(0, col_parts, body, 0)
+                )
+                pl.when(is_root | (r == root_cross))(handed.wait_send)
+                over_x = remote(
+                    col_at(k, h), col_at(k, h), col_send.at[0, 2 * k + h], col_recv.at[0], sib, c
+                )
+                pl.when(is_root)(over_x.wait_send)
+
+        pl.when(k != skip)(act)
+
+    over(0, col_parts, sent)
+    if tuned:
+        pl.when(far)(fine_sent)
 
 
 def store_kernel(ly, lz, group, u_in, white_in, own_in, total_in, u_out, white_out, own_out, score_out, info_out, sem):
@@ -727,8 +825,9 @@
         out_specs=(vmem,) * 4,
         scratch_shapes=[pltpu.VMEM(shape, dtype) for shape, dtype in arrays]
         + [
-            dma((3, 3)), dma((3, prow_size)), dma((3, chunks)), dma((chunks,)),
+            dma((4, 3)), dma((4, prow_size)), dma((3, chunks)), dma((chunks,)),
             dma((2, col_chunks)), dma((col_chunks,)), dma((3,)), dma((prow_size,)), dma((col_chunks + 9,)),
+            dma((2, FINE)), dma((2, FINE)), dma((2, 2, FINE)), dma((2, FINE)), dma((2, FINE)),
         ],
         compiler_params=pltpu.CompilerParams(
             collective_id=0, has_side_effects=True, vmem_limit_bytes=32 * 1024 * 1024

time: 66.8 us -> 63.9 us (0.957)
  Pallas kernels: 65.8 us -> 63 us
    pallas_call x1, Pallas kernels: 61.6 us -> 58.8 us  [local(): pl.pallas_call(functools.partial(main_kernel, ly, lz, pcol_size // prow_s...]
where the time goes in v3:
time: 63.9 us; the launch traced here: 63.8 us
  Pallas kernels  63 us (99%)
  between operations  0.8 us (1%)
    pallas_call x1, Pallas kernels, local(): pl.pallas_call(functools.partial(main_kernel, ly, lz, pcol_size // prow_s...  58.8 us
    pallas_call x1, Pallas kernels, local(): pl.pallas_call(functools.partial(store_kernel, ly, lz, pcol_size // prow_...  4.21 us

profile of v3, /device:TPU:7, one launch (start us, length us, event | category | flops | bytes accessed | tf_op | source)
XLA Modules:
  0.0 63.8 jit_solution(11763335003659629361)
XLA Ops:
  0.6 58.8 %shard_map.110 = (f32[2048,1024]{1,0:T(8,128)S(1)}, f32[2048,256]{1,0:T(8,128)S(1)}, f32[256,512]{1,0:T(8,128)S(1)}, f32[8,256]{1,0:T(8,128)S(1)}) custom-call(f32[128,512]{1,0:T(8,128)} %diag_in.1, f32[128,256]{1,0:T(8,128)} %top_in.1, f32[1,128]{1,0:T(1,128)} %bitcast.5, f32[256,512]{1,0:T(8,128)} %panel_in.1, f32[2048,1024]{1,0:T(8,128)} %trailing_in.1, ...), custom_call_target="tpu_custom_call" | custom-call | tf_op jit(solution)/shard_map/pallas_call | solution.py:816
  59.4 4.2 %shard_map.111 = (f32[2048,1024]{1,0:T(8,128)}, f32[2048,256]{1,0:T(8,128)}, f32[256,512]{1,0:T(8,128)}, f32[1,256]{1,0:T(1,128)}, f32[1,256]{1,0:T(1,128)}) custom-call(f32[2048,1024]{1,0:T(8,128)S(1)} %get-tuple-element.14.u_in, f32[2048,256]{1,0:T(8,128)S(1)} %get-tuple-element.15.white_in, f32[256,512]{1,0:T(8,128)S(1)} %get-tuple-element.16.own_in, ...), custom_call_target="tpu_custom_call" | custom-call | tf_op jit(solution)/shard_map/pallas_call | solution.py:841

commit v4 on v3

--- a/solution.py
+++ b/solution.py
@@ -10,7 +10,7 @@
 MESH = pl.DeviceIdType.MESH
 HIGHEST = lax.Precision.HIGHEST
 TILE = 16
-FINE = 4
+FINE = 2
 PARTS = 4
 BLOCK = 128
 
@@ -233,9 +233,9 @@
 def main_kernel(
     ly, lz, group,
     diag_in, top_in, pheno_in, panel_in, trailing_in, geno_in, rest_in,
-    u_out, white_out, own_out, total_out,
+    u_out, white_out, own_out, total_out, row_hi, row_lo, y_hi, y_lo,
     a_ref, m_ref, w_ref, row_buf, col_buf, top_buf, pheno_buf, rest_buf,
-    row_hi, row_lo, y_hi, y_lo, g_hi, g_lo, w_hi, w_lo, wt_hi, wt_lo, ai_hi, ai_lo,
+    g_hi, g_lo, w_hi, w_lo, wt_hi, wt_lo, ai_hi, ai_lo,
     stat, stat_buf,
     small_send, small_recv, row_send, row_recv, col_send, col_recv, stat_send, stat_recv, local_sem,
     fine_send, fine_recv, fine_col_send, fine_col_recv, fine_local,
@@ -667,43 +667,37 @@
             arrive(hop_arrivals(3, 1))
             arrive(across_arrivals(2, 1))
 
-        def stage(t):
-            pl.when(t == 0)(first_stage)
-            pl.when(t == 1)(second_stage)
-            pl.when(t < 3)(lambda: row_step(4 + t, pick(row_ids, 4 + t)))
-
-            @pl.when((t < 2) | near)
-            def _():
-                col_step(t, pick(col_ids, t))
-                apply(0, 4, t, 1)
-
         def last_rows():
-            pl.when(low_end | high_end)(fine_arrive)
+            pl.when((low_end | high_end) & near)(fine_arrive)
             row_step(7, row_ids[7])
             send_stats()
 
-        def rest(k):
-            pl.when((k == 5) & far)(lambda: cols_ready(col_ids[2]))
-            pl.when(near)(lambda: apply(k, 1, 0, 4))
-            pl.when(far)(lambda: apply(k, 1, 0, 2))
+        def last_column():
+            spare()
+            fine_ready()
+
+        def spare():
+            def one(k):
+                pl.when((k == 7) & (r == root_cross))(fine_hand)
+                apply(k, 1, 0, 2)
+
+            over(4, 8, one)
+
+        def stage(t):
+            pl.when(t == 1)(second_stage)
+            pl.when((t == 2) & far & (low_end | high_end))(fine_arrive)
+            pl.when(t < 3)(lambda: row_step(4 + t, pick(row_ids, 4 + t)))
+            pl.when(((t == 3) & near) | ((t == 2) & far))(last_rows)
+            unit_at = pick(col_ids, t)
+            pl.when((t < 3) | near)(lambda: cols_ready(unit_at))
+            pl.when((t == 3) & far)(last_column)
+            col_step(t, unit_at, False)
+            apply(0, 4, t, 1)
 
         prepare()
+        first_stage()
         over(0, 4, lambda k: row_step(k, pick(row_ids, k)))
         over(0, 4, stage)
-        last_rows()
-        over(4, 8, rest)
-
-        def late_column(t):
-            pl.when(t == 3)(fine_ready)
-            col_step(t, pick(col_ids, t), False)
-
-            def part_of_rows(g):
-                pl.when((t == 2) & (g == 1) & (r == root_cross))(fine_hand)
-                apply(4 * g, 4, t, 1)
-
-            over(0, 2, part_of_rows)
-
-        pl.when(far)(lambda: over(2, 4, late_column))
     else:
         for t in range(5, count + 2):
             event(t)()
@@ -767,23 +761,55 @@
         pl.when(far)(fine_sent)
 
 
-def store_kernel(ly, lz, group, u_in, white_in, own_in, total_in, u_out, white_out, own_out, score_out, info_out, sem):
+def store_kernel(
+    ly, lz, group,
+    u_in, white_in, own_in, total_in, row_hi, row_lo, y_hi, y_lo,
+    u_out, white_out, own_out, score_out, info_out,
+    held, sem, row_sem,
+):
     c = lax.axis_index("pcol")
     rows_piece = own_in.shape[0]
     col_parts = u_in.shape[1] // rows_piece
     tuned = is_tuned(lz, rows_piece, col_parts)
-    row_ids, col_ids = None, None
-    if tuned:
-        _, row_ids, col_ids = orders(ly, lz, lax.rem(c, group) * col_parts, c // ly, lax.rem(c, ly))
-    grid_copies(tuned, u_out, u_in, row_ids, col_ids, rows_piece, True, sem.at[0])
     pairs = [(own_in, own_out), (white_in, white_out)]
     pairs += [(total_in.at[0:1], score_out), (total_in.at[1:2], info_out)]
     copies = [pltpu.make_async_copy(src, dst, sem.at[1 + k]) for k, (src, dst) in enumerate(pairs)]
+    if not tuned:
+        copies.append(pltpu.make_async_copy(u_in, u_out, sem.at[0]))
+        for copy in copies:
+            copy.start()
+        for copy in copies:
+            copy.wait()
+        return
+    far, row_ids, col_ids = orders(ly, lz, lax.rem(c, group) * col_parts, c // ly, lax.rem(c, ly))
+    near = jnp.logical_not(far)
+
+    def span(k):
+        return pl.ds(pl.multiple_of(k * rows_piece, rows_piece), rows_piece)
+
+    def store_row(k, src, at, row_at, cols=range(4)):
+        for j in cols:
+            pltpu.make_async_copy(
+                src.at[span(at), span(j)], u_out.at[span(pick(row_ids, k)), span(col_ids[j])], row_at
+            ).start()
+
+    over(0, 4, lambda k: store_row(k, u_in, k, row_sem.at[k]))
     for copy in copies:
         copy.start()
+
+    pl.when(far)(lambda: over(4, 8, lambda k: store_row(k, u_in, k, row_sem.at[k], (0, 1))))
+
+    def later(k, start):
+        at, cols = span(k), pl.ds(start * rows_piece, (4 - start) * rows_piece)
+        moved = dot3((row_hi[at, :], row_lo[at, :]), (y_hi[:, cols], y_lo[:, cols]), INNER)
+        held[span(k - 4), cols] = u_in[at, cols] - moved
+        store_row(k, held, k - 4, row_sem.at[k], range(start, 4))
+
+    pl.when(near)(lambda: over(4, 8, lambda k: later(k, 0)))
+    pl.when(far)(lambda: over(4, 8, lambda k: later(k, 2)))
     for copy in copies:
         copy.wait()
-    pltpu.make_async_copy(u_in, u_out, sem.at[0]).wait()
+    over(0, 8, lambda k: pltpu.make_async_copy(held.at[span(0), :], u_out.at[span(0), :], row_sem.at[k]).wait())
 
 
 def local(diag_block, panel_cols, trailing, geno_top, geno_rest, pheno_top, pheno_rest):
@@ -807,8 +833,6 @@
         ((row_count, width), f32), ((col_count, width), f32),
         ((prow_size, height, variants), f32), ((prow_size, 1, height), f32),
         ((row_count // unit, 1, unit), f32),
-        ((row_count, width), bf16), ((row_count, width), bf16),
-        ((width, col_count), bf16), ((width, col_count), bf16),
         ((width, wide), bf16), ((width, wide), bf16),
     ]
     arrays += [((width, width), bf16)] * 6
@@ -820,9 +844,13 @@
             pltpu.VMEM(geno_rest.shape, f32),
             pltpu.VMEM(panel_cols.shape, f32),
             pltpu.VMEM(stats, f32),
+            pltpu.VMEM((row_count, width), bf16),
+            pltpu.VMEM((row_count, width), bf16),
+            pltpu.VMEM((width, col_count), bf16),
+            pltpu.VMEM((width, col_count), bf16),
         ),
         in_specs=[hbm] * 7,
-        out_specs=(vmem,) * 4,
+        out_specs=(vmem,) * 8,
         scratch_shapes=[pltpu.VMEM(shape, dtype) for shape, dtype in arrays]
         + [
             dma((4, 3)), dma((4, prow_size)), dma((3, chunks)), dma((chunks,)),
@@ -847,10 +875,12 @@
             jax.ShapeDtypeStruct((1, variants), f32),
             jax.ShapeDtypeStruct((1, variants), f32),
         ),
-        in_specs=[vmem] * 4,
+        in_specs=[vmem] * 8,
         out_specs=(hbm,) * 5,
-        scratch_shapes=[dma((5,))],
-        compiler_params=pltpu.CompilerParams(vmem_limit_bytes=1024 * 1024),
+        scratch_shapes=[
+            pltpu.VMEM((row_count // 2, col_count), f32), dma((5,)), dma((8,)),
+        ],
+        compiler_params=pltpu.CompilerParams(vmem_limit_bytes=12 * 1024 * 1024),
     )(*(pltpu.with_memory_space_constraint(value, pltpu.VMEM) for value in held)))
     return (updated_block, own_factor, white_geno, score.reshape(variants), info.reshape(variants))
 

time: 63.9 us -> 63 us (0.986)
  Pallas kernels: 63 us -> 62 us
    pallas_call x1, Pallas kernels: 58.8 us -> 57.8 us  [local(): pl.pallas_call(functools.partial(main_kernel, ly, lz, pcol_size // prow_s...]
where the time goes in v4:
time: 63 us; the launch traced here: 62.8 us
  Pallas kernels  62 us (98%)
  between operations  0.8 us (1%)
    pallas_call x1, Pallas kernels, local(): pl.pallas_call(functools.partial(main_kernel, ly, lz, pcol_size // prow_s...  57.8 us
    pallas_call x1, Pallas kernels, local(): pl.pallas_call(functools.partial(store_kernel, ly, lz, pcol_size // prow_...  4.22 us

profile of v4, /device:TPU:7, one launch (start us, length us, event | category | flops | bytes accessed | tf_op | source)
XLA Modules:
  0.0 62.8 jit_solution(13689590157254016979)
XLA Ops:
  0.6 57.8 %shard_map.110 = (f32[2048,1024]{1,0:T(8,128)S(1)}, f32[2048,256]{1,0:T(8,128)S(1)}, f32[256,512]{1,0:T(8,128)S(1)}, f32[8,256]{1,0:T(8,128)S(1)}, bf16[2048,512...) custom-call(f32[128,512]{1,0:T(8,128)} %diag_in.1, ...), custom_call_target="tpu_custom_call" | custom-call | tf_op jit(solution)/shard_map/pallas_call | solution.py:840
  58.5 4.2 %shard_map.111 = (f32[2048,1024]{1,0:T(8,128)}, f32[2048,256]{1,0:T(8,128)}, f32[256,512]{1,0:T(8,128)}, f32[1,256]{1,0:T(1,128)}, f32[1,256]{1,0:T(1,128)}) custom-call(f32[2048,1024]{1,0:T(8,128)S(1)} %get-tuple-element.18.u_in, f32[2048,256]{1,0:T(8,128)S(1)} %get-tuple-element.19.white_in, f32[256,512]{1,0:T(8,128)S(1)} %get-tuple-element.20.own_in, ...), custom_call_target="tpu_custom_call" | custom-call | tf_op jit(solution)/shard_map/pallas_call | solution.py:869

commit v5 on v4

--- a/solution.py
+++ b/solution.py
@@ -692,7 +692,7 @@
             pl.when((t < 3) | near)(lambda: cols_ready(unit_at))
             pl.when((t == 3) & far)(last_column)
             col_step(t, unit_at, False)
-            apply(0, 4, t, 1)
+            pl.when((t < 3) | near)(lambda: apply(0, 4, t, 1))
 
         prepare()
         first_stage()
@@ -793,7 +793,8 @@
                 src.at[span(at), span(j)], u_out.at[span(pick(row_ids, k)), span(col_ids[j])], row_at
             ).start()
 
-    over(0, 4, lambda k: store_row(k, u_in, k, row_sem.at[k]))
+    over(0, 4, lambda k: store_row(k, u_in, k, row_sem.at[k], range(3)))
+    pl.when(near)(lambda: over(0, 4, lambda k: store_row(k, u_in, k, row_sem.at[k], (3,))))
     for copy in copies:
         copy.start()
 
@@ -805,6 +806,15 @@
         held[span(k - 4), cols] = u_in[at, cols] - moved
         store_row(k, held, k - 4, row_sem.at[k], range(start, 4))
 
+    def corner(k):
+        at, cols = span(k), pl.ds(3 * rows_piece, rows_piece)
+        moved = dot3((row_hi[at, :], row_lo[at, :]), (y_hi[:, cols], y_lo[:, cols]), INNER)
+        held[at, :rows_piece] = u_in[at, cols] - moved
+        pltpu.make_async_copy(
+            held.at[at, pl.ds(0, rows_piece)], u_out.at[span(pick(row_ids, k)), span(col_ids[3])], row_sem.at[k]
+        ).start()
+
+    pl.when(far)(lambda: over(0, 4, corner))
     pl.when(near)(lambda: over(4, 8, lambda k: later(k, 0)))
     pl.when(far)(lambda: over(4, 8, lambda k: later(k, 2)))
     for copy in copies:

time: 63 us -> 61.4 us (0.975)
  Pallas kernels: 62 us -> 60.5 us
    pallas_call x1, Pallas kernels: 57.8 us -> 55.6 us  [local(): pl.pallas_call(functools.partial(main_kernel, ly, lz, pcol_size // prow_s...]
    pallas_call x1, Pallas kernels: 4.22 us -> 4.92 us  [local(): pl.pallas_call(functools.partial(store_kernel, ly, lz, pcol_size // prow_...]
where the time goes in v5:
time: 61.4 us; the launch traced here: 61.3 us
  Pallas kernels  60.5 us (99%)
  between operations  0.8 us (1%)
    pallas_call x1, Pallas kernels, local(): pl.pallas_call(functools.partial(main_kernel, ly, lz, pcol_size // prow_s...  55.6 us
    pallas_call x1, Pallas kernels, local(): pl.pallas_call(functools.partial(store_kernel, ly, lz, pcol_size // prow_...  4.92 us

profile of v5, /device:TPU:7, one launch (start us, length us, event | category | flops | bytes accessed | tf_op | source)
XLA Modules:
  0.0 61.3 jit_solution(3034779409476735312)
XLA Ops:
  0.6 55.6 %shard_map.110 = (f32[2048,1024]{1,0:T(8,128)S(1)}, f32[2048,256]{1,0:T(8,128)S(1)}, f32[256,512]{1,0:T(8,128)S(1)}, f32[8,256]{1,0:T(8,128)S(1)}, bf16[2048,512...) custom-call(f32[128,512]{1,0:T(8,128)} %diag_in.1, ...), custom_call_target="tpu_custom_call" | custom-call | tf_op jit(solution)/shard_map/pallas_call | solution.py:850
  56.2 4.9 %shard_map.111 = (f32[2048,1024]{1,0:T(8,128)}, f32[2048,256]{1,0:T(8,128)}, f32[256,512]{1,0:T(8,128)}, f32[1,256]{1,0:T(1,128)}, f32[1,256]{1,0:T(1,128)}) custom-call(f32[2048,1024]{1,0:T(8,128)S(1)} %get-tuple-element.18.u_in, f32[2048,256]{1,0:T(8,128)S(1)} %get-tuple-element.19.white_in, f32[256,512]{1,0:T(8,128)S(1)} %get-tuple-element.20.own_in, ...), custom_call_target="tpu_custom_call" | custom-call | tf_op jit(solution)/shard_map/pallas_call | solution.py:879

commit v6 on v5

--- a/solution.py
+++ b/solution.py
@@ -10,7 +10,7 @@
 MESH = pl.DeviceIdType.MESH
 HIGHEST = lax.Precision.HIGHEST
 TILE = 16
-FINE = 2
+FINE = 4
 PARTS = 4
 BLOCK = 128
 

time: 61.4 us -> 61.6 us (level)
  no operation moved by 1% of the time
where the time goes in v6:
time: 61.6 us; the launch traced here: 61.4 us
  Pallas kernels  60.6 us (98%)
  between operations  0.8 us (1%)
    pallas_call x1, Pallas kernels, local(): pl.pallas_call(functools.partial(main_kernel, ly, lz, pcol_size // prow_s...  55.7 us
    pallas_call x1, Pallas kernels, local(): pl.pallas_call(functools.partial(store_kernel, ly, lz, pcol_size // prow_...  4.92 us

profile of v6, /device:TPU:7, one launch (start us, length us, event | category | flops | bytes accessed | tf_op | source)
XLA Modules:
  0.0 61.4 jit_solution(809132738163612906)
XLA Ops:
  0.6 55.7 %shard_map.110 = (f32[2048,1024]{1,0:T(8,128)S(1)}, f32[2048,256]{1,0:T(8,128)S(1)}, f32[256,512]{1,0:T(8,128)S(1)}, f32[8,256]{1,0:T(8,128)S(1)}, bf16[2048,512...) custom-call(f32[128,512]{1,0:T(8,128)} %diag_in.1, ...), custom_call_target="tpu_custom_call" | custom-call | tf_op jit(solution)/shard_map/pallas_call | solution.py:850
  56.3 4.9 %shard_map.111 = (f32[2048,1024]{1,0:T(8,128)}, f32[2048,256]{1,0:T(8,128)}, f32[256,512]{1,0:T(8,128)}, f32[1,256]{1,0:T(1,128)}, f32[1,256]{1,0:T(1,128)}) custom-call(f32[2048,1024]{1,0:T(8,128)S(1)} %get-tuple-element.18.u_in, f32[2048,256]{1,0:T(8,128)S(1)} %get-tuple-element.19.white_in, f32[256,512]{1,0:T(8,128)S(1)} %get-tuple-element.20.own_in, ...), custom_call_target="tpu_custom_call" | custom-call | tf_op jit(solution)/shard_map/pallas_call | solution.py:879
